TPU v7x, 128 devices: a whole 4x4x4 slice. The times are simulated.
128 devices in a mesh: group: 8 (over z, core), ingroup: 16 (over x, y).
Axes of the slice: x: 4, y: 4, z: 4, core: 2. Of those that a mesh axis runs over, the one named last changes fastest.
Arguments:
- hidden_in: bfloat16 [1024, 7168], P(('group', 'ingroup')), may hold values from -6 to 6
- queries: bfloat16 [1024, 64, 576], P(('group', 'ingroup')), may hold values from -20 to 20
- node_latent: bfloat16 [1024, 576], P(('group', 'ingroup')), may hold values from -8 to 8
- cache: bfloat16 [128, 1024, 576], P(('group', 'ingroup')), may hold values from -4 to 4
- cache_len: int32 [128], P(('group', 'ingroup')), may hold values from 512 to 1024
- parents: int32 [128, 8], P(('group', 'ingroup')), may hold values from 0 to 6, as said below
- value_up: bfloat16 [64, 512, 128], P('ingroup'), may hold values from -0.25 to 0.25
- out_proj: bfloat16 [8192, 7168], P('ingroup'), may hold values from -0.0625 to 0.0625
- ffn_gain: float32 [7168], replicated, may hold values from 0.1 to 1.9
- route_experts: int32 [1024, 8], P(('group', 'ingroup')), may hold values from 0 to 31, as said below
- route_weights: float32 [1024, 8], P(('group', 'ingroup')), may hold values from 0.1 to 0.6
- expert_gate: bfloat16 [128, 7168, 256], P(('group', 'ingroup')), may hold values from -0.0625 to 0.0625
- expert_up: bfloat16 [128, 7168, 256], P(('group', 'ingroup')), may hold values from -0.0625 to 0.0625
- expert_down: bfloat16 [128, 256, 7168], P(('group', 'ingroup')), may hold values from -0.1875 to 0.1875
- shared_gate: bfloat16 [7168, 1024], P(None, 'ingroup'), may hold values from -0.0625 to 0.0625
- shared_up: bfloat16 [7168, 1024], P(None, 'ingroup'), may hold values from -0.0625 to 0.0625
- shared_down: bfloat16 [1024, 7168], P('ingroup'), may hold values from -0.1875 to 0.1875
Outputs:
- mixed: bfloat16 [1024, 7168], P(('group', 'ingroup'))
Inputs may be any that keep to these rules, and one draw needn't show every extreme that they name: `parents`: the parent of node n is a node below n; the root, node 0, has parent 0. `route_experts`: each row names 8 different experts, two in each of 4 node groups, expert e belonging to node group e // 4; over the rows of one device no expert is named more than 4 times.
All inputs are finite; a program needn't handle non-finite values.
Results may differ from a plain program's by a relative error of at most 0.023.
Values may be sent and summed in bfloat16 or wider, within the bound.
A program may use at most 128 MiB of HBM per device.

v0:
```python
import jax
import jax.numpy as jnp
from jax import lax
from jax.sharding import PartitionSpec as P

SPLIT = 4


SCALE_QK = 192.0 ** (-0.5)
NORM_EPS = 1e-06


def ancestors(parents):
    node_count = parents.shape[-1]
    node_ids = jnp.arange(node_count, dtype=jnp.int32)
    pointer = jnp.broadcast_to(node_ids, parents.shape)
    visible = pointer[..., :, None] == node_ids
    for hop_index in range(node_count - 1):
        pointer = jnp.take_along_axis(parents, pointer, axis=-1)
        visible = visible | (pointer[..., :, None] == node_ids)
    return visible.astype(jnp.int32)


def attend(queries, node_keys, cache, cache_len, visible, latent_width):
    cache_scores = (
        jnp.einsum("bnhc,blc->bnhl", queries, cache, preferred_element_type=jnp.float32) * SCALE_QK
    )
    node_scores = (
        jnp.einsum("bnhc,bmc->bnhm", queries, node_keys, preferred_element_type=jnp.float32)
        * SCALE_QK
    )
    positions = jnp.arange(cache.shape[1], dtype=jnp.int32)
    cache_live = positions[None, :] < cache_len[:, None]
    cache_scores = jnp.where(cache_live[:, None, None, :], cache_scores, -jnp.inf)
    node_scores = jnp.where((visible != 0)[:, :, None, :], node_scores, -jnp.inf)
    highest = jnp.maximum(jnp.max(cache_scores, axis=-1), jnp.max(node_scores, axis=-1))[..., None]
    cache_exp = jnp.exp(cache_scores - highest)
    node_exp = jnp.exp(node_scores - highest)
    exp_total = jnp.sum(cache_exp, axis=-1, keepdims=True) + jnp.sum(
        node_exp, axis=-1, keepdims=True
    )
    cache_weights = (cache_exp / exp_total).astype(jnp.bfloat16)
    node_weights = (node_exp / exp_total).astype(jnp.bfloat16)
    latent = jnp.einsum(
        "bnhl,blc->bnhc",
        cache_weights,
        cache[:, :, :latent_width],
        preferred_element_type=jnp.float32,
    )
    latent = latent + jnp.einsum(
        "bnhm,bmc->bnhc",
        node_weights,
        node_keys[:, :, :latent_width],
        preferred_element_type=jnp.float32,
    )
    return latent.astype(jnp.bfloat16)


def rms_normed(row_block, norm_gain):
    widened = row_block.astype(jnp.float32)
    mean_square = jnp.mean(widened * widened, axis=-1, keepdims=True)
    return (widened * lax.rsqrt(mean_square + NORM_EPS) * norm_gain).astype(jnp.bfloat16)


def shared_hidden_of(row_block, shared_gate, shared_up):
    gate_part = jnp.dot(row_block, shared_gate, preferred_element_type=jnp.float32)
    up_part = jnp.dot(row_block, shared_up, preferred_element_type=jnp.float32)
    return (jax.nn.silu(gate_part) * up_part).astype(jnp.bfloat16)


def expert_ffn(received, expert_gate, expert_up, expert_down):
    gate_part = jnp.einsum(
        "scd,df->scf", received, expert_gate[0], preferred_element_type=jnp.float32
    )
    up_part = jnp.einsum("scd,df->scf", received, expert_up[0], preferred_element_type=jnp.float32)
    hidden = (jax.nn.silu(gate_part) * up_part).astype(jnp.bfloat16)
    return jnp.einsum(
        "scf,fd->scd", hidden, expert_down[0], preferred_element_type=jnp.float32
    ).astype(jnp.bfloat16)


def local(
    hidden_in,
    queries,
    node_latent,
    cache,
    cache_len,
    parents,
    value_up,
    out_proj,
    ffn_gain,
    route_experts,
    route_weights,
    expert_gate,
    expert_up,
    expert_down,
    shared_gate,
    shared_up,
    shared_down,
):
    req_count, cache_size, query_width = cache.shape
    node_count = parents.shape[1]
    row_count = queries.shape[0]
    head_count = queries.shape[1]
    latent_width = value_up.shape[1]
    model_width = hidden_in.shape[1]
    visible = ancestors(parents)
    latent = attend(
        queries.reshape(req_count, node_count, head_count, query_width),
        node_latent.reshape(req_count, node_count, query_width),
        cache,
        cache_len,
        visible,
        latent_width,
    )
    latent = latent.reshape(row_count, head_count, latent_width)
    by_head = lax.all_to_all(latent, "ingroup", split_axis=1, concat_axis=0, tiled=True)
    head_out = jnp.einsum(
        "rhc,hcv->rhv", by_head, value_up, preferred_element_type=jnp.float32
    ).astype(jnp.bfloat16)
    head_flat = head_out.reshape(head_out.shape[0], -1)
    attention_out = lax.psum_scatter(
        jnp.dot(head_flat, out_proj, preferred_element_type=jnp.float32).astype(jnp.bfloat16),
        "ingroup",
        scatter_dimension=0,
        tiled=True,
    ).astype(jnp.float32)
    attended = (hidden_in.astype(jnp.float32) + attention_out).astype(jnp.bfloat16)
    normed = rms_normed(attended, ffn_gain)
    shared_hidden = shared_hidden_of(
        lax.all_gather(normed, "ingroup", axis=0, tiled=True), shared_gate, shared_up
    )
    shared_out = lax.psum_scatter(
        jnp.dot(shared_hidden, shared_down, preferred_element_type=jnp.float32).astype(
            jnp.bfloat16
        ),
        "ingroup",
        scatter_dimension=0,
        tiled=True,
    ).astype(jnp.float32)
    group_count = lax.axis_size("group")
    ingroup_count = lax.axis_size("ingroup")
    device_count = group_count * ingroup_count
    group_experts = ingroup_count // SPLIT
    expert_count = group_count * group_experts
    capacity = max(2, (2 * row_count + group_experts - 1) // group_experts)
    top_count = route_experts.shape[1]
    pair_experts = route_experts.reshape(-1)
    pair_ids = jnp.arange(pair_experts.shape[0], dtype=jnp.int32)
    earlier = (pair_experts[:, None] == pair_experts[None, :]) & (
        pair_ids[None, :] < pair_ids[:, None]
    )
    slot_ids = pair_experts * capacity + jnp.sum(earlier.astype(jnp.int32), axis=1)
    slot_total = expert_count * capacity
    placing = (jnp.arange(slot_total, dtype=jnp.int32)[:, None] == slot_ids[None, :]).astype(
        jnp.float32
    )
    placing = jnp.sum(placing.reshape(slot_total, row_count, top_count), axis=2).astype(
        jnp.bfloat16
    )
    send_rows = jnp.dot(placing, normed, preferred_element_type=jnp.float32).astype(jnp.bfloat16)
    send_rows = jnp.broadcast_to(
        send_rows.reshape(expert_count, 1, capacity, model_width),
        (expert_count, SPLIT, capacity, model_width),
    )
    send_rows = send_rows.reshape(device_count, capacity, model_width)
    produced = expert_ffn(
        lax.all_to_all(send_rows, ("group", "ingroup"), split_axis=0, concat_axis=0, tiled=True),
        expert_gate,
        expert_up,
        expert_down,
    )
    returned = lax.all_to_all(
        produced, ("group", "ingroup"), split_axis=0, concat_axis=0, tiled=True
    )
    block_sum = jnp.sum(
        returned.reshape(expert_count, SPLIT, capacity, model_width).astype(jnp.float32), axis=1
    )
    back_rows = block_sum.reshape(slot_total, model_width)
    picked = jnp.take(back_rows, slot_ids, axis=0).reshape(row_count, top_count, model_width)
    routed = jnp.einsum("rk,rkd->rd", route_weights, picked)
    return (attended.astype(jnp.float32) + shared_out + routed).astype(jnp.bfloat16)


def solution(mesh):
    in_specs = (
        P(("group", "ingroup"), None),
        P(("group", "ingroup"), None, None),
        P(("group", "ingroup"), None),
        P(("group", "ingroup"), None, None),
        P(("group", "ingroup")),
        P(("group", "ingroup"), None),
        P("ingroup", None, None),
        P("ingroup", None),
        P(),
        P(("group", "ingroup"), None),
        P(("group", "ingroup"), None),
        P(("group", "ingroup"), None, None),
        P(("group", "ingroup"), None, None),
        P(("group", "ingroup"), None, None),
        P(None, "ingroup"),
        P(None, "ingroup"),
        P("ingroup", None),
    )
    out_specs = P(("group", "ingroup"), None)
    return jax.shard_map(local, mesh=mesh, in_specs=in_specs, out_specs=out_specs, check_vma=False)
```

profile of v0, /device:TPU:1, one launch (start us, length us, event | category | flops | bytes accessed | tf_op | source)
XLA Modules:
  0.0 461.2 jit_solution(3516916771156196826)
XLA Ops:
  6.6 1.4 gather_fusion.1
  8.0 1.4 gather_fusion.2
  9.5 1.3 gather_fusion.3
  10.8 1.3 gather_fusion.4
  12.1 0.6 gather_fusion.5
  12.8 0.6 gather_fusion.6
  13.5 0.6 gather_fusion.7
  15.3 1.1 fusion.7
  17.1 0.8 fusion.25
  18.5 17.9 %all_to_all.28 = bf16[8,64,512]{2,0,1:T(8,128)(2,1)S(1)} all-to-all(bf16[8,64,512]{2,0,1:T(8,128)(2,1)S(1)} %copy.36), channel_id=1, replica_groups=mesh['group'=8,'ingroup'=16] {'ingroup'}, dimensions={1} | all-to-all | bytes 1048576 | tf_op jit(solution)/shard_map/all_to_all | solution.py:117
  36.9 2.5 convolution_convert_fusion.3
  41.1 86.6 %all-reduce.5.cloned.1.call-done = bf16[128,7168]{1,0:T(8,128)(2,1)} async-done(((bf16[128,7168]{1,0:T(8,128)(2,1)}), bf16[128,7168]{1,0:T(8,128)(2,1)}) %all-reduce.5.cloned.1.call-update) | async-done | bytes 1835024
  127.7 1.1 fusion.33
  128.9 0.7 convolution_convert_fusion.1
  129.6 1.7 broadcast_in_dim.41
  131.3 6.7 %broadcast_in_dim.42 = bf16[32,4,4,7168]{3,2,1,0:T(4,128)(2,1)} broadcast(bf16[32,4,7168]{2,1,0:T(4,128)(2,1)} %broadcast_in_dim.41), dimensions={0,2,3} | broadcast | bytes 9175040 | tf_op jit(solution)/shard_map/broadcast_in_dim | solution.py:162
  137.9 95.5 %all_to_all.29 = bf16[128,4,7168]{2,1,0:T(4,128)(2,1)S(1)} all-to-all(bf16[128,4,7168]{2,1,0:T(4,128)(2,1)} %bitcast.146), channel_id=1, replica_groups=mesh['group'=8,'ingroup'=16] {'group','ingroup'}, dimensions={0} | all-to-all | bytes 14680064 | tf_op jit(solution)/shard_map/all_to_all | solution.py:168
  233.4 4.1 fusion.2
  237.6 4.2 fusion.16
  241.8 5.0 %convolution_convert_fusion = bf16[128,4,7168]{2,0,1:T(8,128)(2,1)} fusion(bf16[128,4,256]{2,0,1:T(8,128)(2,1)S(1)} %fusion.16, bf16[1,256,7168]{2,1,0:T(8,128)(2,1)S(1)} %copy-done.3), kind=kOutput, calls=%fused_computation.9 | convolution fusion | flops 1882718208 | bytes 11272192 | tf_op jit(solution)/shard_map/scf,fd->scd/dot_general | solution.py:77
  246.8 12.0 %copy.41 = bf16[128,4,7168]{2,1,0:T(4,128)(2,1)} copy(bf16[128,4,7168]{2,0,1:T(8,128)(2,1)} %convolution_convert_fusion) | data formatting | bytes 14680064 | tf_op jit(solution)/shard_map/convert_element_type | solution.py:79
  258.8 4.8 %all-to-all-start.2 = ((bf16[128,4,7168]{2,1,0:T(4,128)(2,1)}), bf16[128,4,7168]{2,1,0:T(4,128)(2,1)}, u32[]{:S(2)}, u32[]{:S(2)}) async-start(bf16[128,4,7168]{2,1,0:T(4,128)(2,1)} %copy.41), calls=%async_computation.2 | async-start | bytes 14680064 | tf_op jit(solution)/shard_map/all_to_all | solution.py:173
  263.6 0.7 all-gather.2.cloned.1.call-update
  264.4 90.9 %all-gather.2.cloned.1.call-done = bf16[128,7168]{1,0:T(8,128)(2,1)} async-done(((bf16[8,7168]{1,0:T(8,128)(2,1)}), bf16[128,7168]{1,0:T(8,128)(2,1)}) %all-gather.2.cloned.1.call-update) | async-done | bytes 1835024 | tf_op jit(solution)/shard_map/all_gather | solution.py:131
  355.3 2.6 fusion.73
  357.9 4.7 %convolution_convert_fusion.2 = bf16[128,7168]{1,0:T(8,128)(2,1)} fusion(bf16[64,7168]{1,0:T(8,128)(2,1)S(1)} %copy-done, bf16[128,7168]{1,0:T(8,128)(2,1)S(1)} %copy-done.2, bf16[7168,64]{0,1:T(8,128)(2,1)} %param.34, f32[128,64]{0,1:T(8,128)S(1)} %fusion.73), kind=kOutput, calls=%fused_computation.11 | convolution fusion | flops 235847680 | bytes 5537792 | tf_op jit(solution)/shard_map/dot_general | solution.py:134
  362.8 9.0 %convert_reduce_fusion = bf16[32,4,7168]{2,1,0:T(4,128)(2,1)} fusion(bf16[128,4,7168]{2,1,0:T(4,128)(2,1)} %all-to-all-done.2), kind=kLoop, calls=%fused_computation.8 | loop fusion | flops 6422528 | bytes 9175040 | tf_op jit(solution)/shard_map/reduce_sum | solution.py:176
  371.7 3.0 reshape.403
  374.7 2.1 gather_fusion
  376.8 1.6 fusion.8
  378.4 74.6 %all-reduce.7.cloned.1.call-done = bf16[128,7168]{1,0:T(8,128)(2,1)} async-done(((bf16[128,7168]{1,0:T(8,128)(2,1)}), bf16[128,7168]{1,0:T(8,128)(2,1)}) %all-reduce.7.cloned.1.call-update) | async-done | bytes 1835024
  453.0 1.6 fusion.37
  (80 shorter events, 3.7 us)
Async XLA Ops:
  6.5 351.4 %copy-start = (bf16[64,7168]{1,0:T(8,128)(2,1)S(1)}, bf16[64,7168]{1,0:T(8,128)(2,1)}, u32[]{:S(2)}) copy-start(bf16[64,7168]{1,0:T(8,128)(2,1)} %param.35) | copy-start | bytes 2752516
  6.5 5.6 %copy-start.1 = (s32[1,8]{1,0:T(1,128)S(1)}, s32[1,8]{1,0:T(1,128)}, u32[]{:S(2)}) copy-start(s32[1,8]{1,0:T(1,128)} %param.24) | copy-start | bytes 100
  6.5 8.3 %copy-start.5 = (bf16[8,64,576]{2,1,0:T(8,128)(2,1)S(1)}, bf16[8,64,576]{2,1,0:T(8,128)(2,1)}, u32[]{:S(2)}) copy-start(bf16[8,64,576]{2,1,0:T(8,128)(2,1)} %param.20) | copy-start | bytes 1769476
  6.5 8.3 %copy-start.9 = (bf16[8,576]{1,0:T(8,128)(2,1)S(1)}, bf16[8,576]{1,0:T(8,128)(2,1)}, u32[]{:S(2)}) copy-start(bf16[8,576]{1,0:T(8,128)(2,1)} %param.21) | copy-start | bytes 27652
  6.5 121.2 %all-reduce.5.cloned.1.call-start = ((), (), s32[]{:S(2)}) async-start(), calls=%async_computation.4 | async-start | bytes 3670016
  8.0 7.3 %copy-start.13 = (bf16[1,1024,576]{1,2,0:T(8,128)(2,1)S(1)}, bf16[1,1024,576]{1,2,0:T(8,128)(2,1)}, u32[]{:S(2)}) copy-start(bf16[1,1024,576]{1,2,0:T(8,128)(2,1)} %param.22) | copy-start | bytes 3538948
  17.1 19.8 %slice-start = ((s8[7340032]{0:T(1024)(128)(4,1)}), s8[4194304]{0:T(1024)(128)(4,1)S(1)}, s32[]{:S(2)}) async-start(s8[7340032]{0:T(1024)(128)(4,1)} %bitcast.147), calls=%async_computation.6 | async-start | bytes 8388608
  17.1 19.7 %slice-start.1 = ((s8[7340032]{0:T(1024)(128)(4,1)}), s8[3145728]{0:T(1024)(128)(4,1)S(1)}, s32[]{:S(2)}) async-start(s8[7340032]{0:T(1024)(128)(4,1)} %bitcast.147), calls=%async_computation.7 | async-start | bytes 6291456
  17.9 18.6 %copy-start.6 = (bf16[4,512,128]{2,1,0:T(8,128)(2,1)S(1)}, bf16[4,512,128]{2,1,0:T(8,128)(2,1)}, u32[]{:S(2)}) copy-start(bf16[4,512,128]{2,1,0:T(8,128)(2,1)} %param.25) | copy-start | bytes 1572868
  36.8 2.5 copy-start.8
  36.8 2.9 copy-start.15
  36.9 90.8 %copy-start.7 = (bf16[8,7168]{1,0:T(8,128)(2,1)S(1)}, bf16[8,7168]{1,0:T(8,128)(2,1)}, u32[]{:S(2)}) copy-start(bf16[8,7168]{1,0:T(8,128)(2,1)} %param.19) | copy-start | bytes 344068
  39.3 89.5 %copy-start.10 = (f32[7168]{0:T(1024)S(1)}, f32[7168]{0:T(1024)}, u32[]{:S(2)}) copy-start(f32[7168]{0:T(1024)} %param.27) | copy-start | bytes 86020
  128.9 2.4 copy-start.4
  137.9 95.5 %copy-start.11 = (bf16[1,7168,256]{2,1,0:T(8,128)(2,1)S(1)}, bf16[1,7168,256]{2,1,0:T(8,128)(2,1)}, u32[]{:S(2)}) copy-start(bf16[1,7168,256]{2,1,0:T(8,128)(2,1)} %param.30) | copy-start | bytes 11010052
  233.4 4.1 copy-start.12
  237.6 4.3 copy-start.3
  258.8 103.9 %all-to-all-start.2 = ((bf16[128,4,7168]{2,1,0:T(4,128)(2,1)}), bf16[128,4,7168]{2,1,0:T(4,128)(2,1)}, u32[]{:S(2)}, u32[]{:S(2)}) async-start(bf16[128,4,7168]{2,1,0:T(4,128)(2,1)} %copy.41), calls=%async_computation.2 | async-start | bytes 14680064 | tf_op jit(solution)/shard_map/all_to_all | solution.py:173
  263.6 91.7 %all-gather.2.cloned.1.call-start = ((), (), s32[]{:S(2)}) async-start(), calls=%async_computation.3 | async-start | bytes 1949696 | tf_op jit(solution)/shard_map/all_gather | solution.py:131
  264.3 188.7 %all-reduce.7.cloned.1.call-start = ((), (), s32[]{:S(2)}) async-start(), calls=%async_computation.5 | async-start | bytes 3670016
  355.3 2.6 copy-start.2
  374.7 2.1 copy-start.14
Sparse Core Ops, SparseCore 0:
  39.5 88.1 all-reduce.4
  266.6 88.6 all-gather.1
  362.8 90.2 all-reduce.6
where the time goes:
time: 462 us; the launch traced here: 461 us
  waiting for transfers between devices  253 us (55%)
  blocking collectives  113 us (24%)
  local copies, waits for them, and re-layouts  33.9 us (7%)
  matrix products  28.4 us (6%)
  between operations  14.9 us (3%)
  other arithmetic  12.8 us (3%)
  starting transfers between devices  4.89 us (1%)
    unnamed x5, waiting for transfers between devices  162 us
    all_to_all x1, blocking collectives, local(): lax.all_to_all(send_rows, ('group', 'ingroup'), split_axis=0, concat_axis...  95.5 us
    all_gather x1, waiting for transfers between devices, local(): lax.all_gather(normed, 'ingroup', axis=0, tiled=True)  90.9 us
    all_to_all x1, blocking collectives, local(): lax.all_to_all(latent, 'ingroup', split_axis=1, concat_axis=0, tiled=True)  17.9 us
    convert_element_type x1, local copies, waits for them, and re-layouts, expert_ffn(): return jnp.einsum('scf,fd->scd', hidden, expert_down[0], preferred_elemen...  12 us
  transfers between devices with their start and end apart: 4, of which 3 were waited for; matrix products, arithmetic and copies ran while one was open for 5% of the time, Pallas kernels for 0%

commit v1 on v0

v1 whole, which is shorter than its diff:
```python
import functools

import jax
import jax.numpy as jnp
from jax import lax
from jax.experimental import pallas as pl
from jax.experimental.pallas import tpu as pltpu
from jax.sharding import PartitionSpec as P

MESH = pl.DeviceIdType.MESH
F32 = jnp.float32
BF16 = jnp.bfloat16
SCALE_QK = 192.0 ** (-0.5)
NORM_EPS = 1e-06
RING = 4
CORES = 2
LANES = 128
AXES = ("z", "x", "y")
GATHER_ORDERS = (("x", "y", "z"), ("y", "z", "x"), ("z", "x", "y"))
SCATTER_ORDERS = (("z", "x", "y"), ("x", "y", "z"), ("y", "z", "x"))
PLANE_ORDERS = (("x", "y"), ("y", "x"))


def column_parts(width, count):
    tiles = width // LANES
    sizes = [tiles // count + (1 if k < tiles % count else 0) for k in range(count)]
    parts, start = [], 0
    for size in sizes:
        parts.append((start * LANES, size * LANES))
        start += size
    return tuple(parts)


def my_position():
    group, inner = lax.axis_index("group"), lax.axis_index("ingroup")
    return {
        "z": lax.div(group, CORES),
        "core": lax.rem(group, CORES),
        "x": lax.div(inner, RING),
        "y": lax.rem(inner, RING),
    }


def device_at(pos):
    return (pos["z"] * CORES + pos["core"], pos["x"] * RING + pos["y"])


def moved(pos, axis, by):
    other = dict(pos)
    other[axis] = lax.rem(pos[axis] + (by % RING), RING)
    return other


def sibling_of(pos):
    other = dict(pos)
    other["core"] = 1 - pos["core"]
    return other


def greet(devices):
    barrier = pltpu.get_barrier_semaphore()
    for device in devices:
        pl.semaphore_signal(barrier, inc=1, device_id=device, device_id_type=MESH)
    pl.semaphore_wait(barrier, len(devices))


class Copies:
    def __init__(self, send_sems, recv_sems):
        self.send_sems, self.recv_sems, self.started = send_sems, recv_sems, []

    def start(self, src, dst, device):
        slot = len(self.started)
        copy = pltpu.make_async_remote_copy(
            src_ref=src,
            dst_ref=dst,
            send_sem=self.send_sems.at[slot],
            recv_sem=self.recv_sems.at[slot],
            device_id=device,
            device_id_type=MESH,
        )
        copy.start()
        self.started.append(copy)
        return copy

    def finish(self):
        for copy in self.started:
            copy.wait_send()


def view_index(axes, fixed, split_axis, half, columns):
    index = []
    for axis in axes:
        if axis in fixed:
            index.append(fixed[axis])
        elif axis == split_axis and half is not None:
            index.append(pl.ds(half * (RING // 2), RING // 2))
        else:
            index.append(slice(None))
    index.append(slice(None))
    if split_axis is None and half is not None:
        low = (columns // LANES + 1) // 2 * LANES
        index.append(pl.ds(0, low) if half == 0 else pl.ds(low, columns - low))
    else:
        index.append(slice(None))
    return tuple(index)


class Gather:
    def __init__(self, copies, pos, ref, order):
        self.copies, self.pos, self.ref, self.order = copies, pos, ref, order
        self.columns = ref.shape[-1]

    def view(self, place, half):
        fixed = {axis: self.pos[axis] for axis in self.order[self.phase + 1 :]}
        fixed[self.axis] = place
        split_axis = self.order[0] if self.phase else None
        return self.ref.at[view_index(AXES, fixed, split_axis, half, self.columns)]

    def begin(self, phase):
        self.phase, self.axis = phase, self.order[phase]
        pos, axis = self.pos, self.axis
        self.plus, self.minus = device_at(moved(pos, axis, 1)), device_at(moved(pos, axis, -1))
        own = [self.view(pos[axis], half) for half in (0, 1)]
        self.first = [
            self.copies.start(own[0], own[0], self.plus),
            self.copies.start(own[1], own[1], self.minus),
            self.copies.start(own[1], own[1], self.plus),
            self.copies.start(own[0], own[0], self.minus),
        ]

    def relay(self):
        below = moved(self.pos, self.axis, -1)[self.axis]
        above = moved(self.pos, self.axis, 1)[self.axis]
        self.first[0].wait_recv()
        low = self.view(below, 0)
        self.far = [self.copies.start(low, low, self.plus)]
        self.first[1].wait_recv()
        high = self.view(above, 1)
        self.far.append(self.copies.start(high, high, self.minus))

    def wait_near(self):
        self.first[2].wait_recv()
        self.first[3].wait_recv()

    def wait_far(self):
        self.far[0].wait_recv()
        self.far[1].wait_recv()


class Scatter:
    def __init__(self, copies, pos, axes, ref, order, landing):
        self.copies, self.pos, self.axes, self.ref = copies, pos, axes, ref
        self.order, self.landing = order, landing
        self.columns = ref.shape[-1]

    def begin(self, phase):
        self.phase, self.axis = phase, self.order[phase]
        self.later = tuple(axis for axis in self.axes if axis in self.order[phase + 1 :])
        self.split_axis = self.order[-1] if self.later else None
        self.relayed, self.from_minus, self.from_plus = self.landing[phase]
        pos, axis = self.pos, self.axis
        self.above, self.below = moved(pos, axis, 1)[axis], moved(pos, axis, -1)[axis]
        self.across = moved(pos, axis, 2)[axis]
        self.plus, self.minus = device_at(moved(pos, axis, 1)), device_at(moved(pos, axis, -1))

    def fixed(self, place):
        fixed = {axis: self.pos[axis] for axis in self.order[: self.phase]}
        fixed[self.axis] = place
        return fixed

    def block(self, place, half):
        return self.ref.at[
            view_index(self.axes, self.fixed(place), self.split_axis, half, self.columns)
        ]

    def landed(self, ref, half):
        return ref.at[view_index(self.later, {}, self.split_axis, half, self.columns)]

    def send_far(self):
        start = self.copies.start
        self.far = [
            start(self.block(self.across, 0), self.landed(self.relayed, 0), self.plus),
            start(self.block(self.across, 1), self.landed(self.relayed, 1), self.minus),
        ]

    def send_near(self):
        start = self.copies.start
        self.near = [
            start(self.block(self.above, 1), self.landed(self.from_minus, 1), self.plus),
            start(self.block(self.below, 0), self.landed(self.from_plus, 0), self.minus),
        ]

    def add_into(self, place, half, refs):
        if not self.later:
            block = view_index(self.axes, self.fixed(place), None, half, self.columns)
            land = view_index((), {}, None, half, self.columns)
            total = self.ref[block].astype(F32)
            for ref in refs:
                total += ref[land].astype(F32)
            self.ref[block] = total.astype(BF16)
            return
        spans = [
            RING // 2 if axis == self.split_axis and half is not None else RING
            for axis in self.later
        ]
        steps = 1
        for span in spans:
            steps *= span

        def slab(step, carry):
            places, rest = {}, step
            for axis, span in reversed(list(zip(self.later, spans))):
                place_in = lax.rem(rest, span)
                rest = lax.div(rest, span)
                if axis == self.split_axis and half is not None:
                    place_in = place_in + half * (RING // 2)
                places[axis] = place_in
            land = tuple(places[axis] for axis in self.later)
            both = dict(places)
            both.update(self.fixed(place))
            block = tuple(both[axis] for axis in self.axes)
            total = self.ref[block].astype(F32)
            for ref in refs:
                total += ref[land].astype(F32)
            self.ref[block] = total.astype(BF16)
            return carry

        lax.fori_loop(0, steps, slab, 0)

    def relay(self):
        start = self.copies.start
        self.far[0].wait_recv()
        self.add_into(self.above, 0, [self.relayed])
        self.near.append(
            start(self.block(self.above, 0), self.landed(self.from_minus, 0), self.plus)
        )
        self.far[1].wait_recv()
        self.add_into(self.below, 1, [self.relayed])
        self.near.append(
            start(self.block(self.below, 1), self.landed(self.from_plus, 1), self.minus)
        )

    def wait_near(self):
        for copy in self.near:
            copy.wait_recv()

    def finish(self):
        self.wait_near()
        self.add_into(self.pos[self.axis], None, [self.from_minus, self.from_plus])

    def finish_last(self):
        self.wait_near()
        block = tuple(self.pos[axis] for axis in self.axes)
        total = self.ref[block].astype(F32)
        return total + self.from_minus[...].astype(F32) + self.from_plus[...].astype(F32)


def landing_shapes(axis_count, rows, columns):
    shapes = []
    for phase in range(axis_count):
        lead = (RING,) * (axis_count - 1 - phase)
        shapes += [pltpu.VMEM(lead + (rows, columns), BF16)] * 3
    return shapes


def by_phase(refs):
    return [refs[3 * k : 3 * k + 3] for k in range(len(refs) // 3)]


def attention_kernel(
    latent_ref,
    value_up_ref,
    out_proj_hbm,
    hidden_ref,
    gain_ref,
    attended_ref,
    normed_ref,
    latents,
    proj,
    head_out,
    residual,
    hidden_away,
    squares,
    squares_in,
    part_refs,
    landing_refs,
    send_sems,
    recv_sems,
    local_sem,
):
    pos = my_position()
    core, group, inner = pos["core"], lax.axis_index("group"), lax.axis_index("ingroup")
    sibling = device_at(sibling_of(pos))
    rows = hidden_ref.shape[0]
    half = normed_ref.shape[1]
    model_width = hidden_ref.shape[1]
    inner_count = latent_ref.shape[0]
    head_count, latent_width, value_width = value_up_ref.shape
    mine = pl.ds(pl.multiple_of(core * half, LANES), half)
    other = pl.ds(pl.multiple_of((1 - core) * half, LANES), half)
    load_proj = pltpu.make_async_copy(out_proj_hbm.at[:, mine], proj, local_sem)
    load_proj.start()
    peers = [lax.rem(inner + step, inner_count) for step in range(1, inner_count)]
    greet([(group, peer) for peer in peers] + [sibling])
    copies = Copies(send_sems, recv_sems)

    arrivals = [
        copies.start(latent_ref.at[peer], latents.at[inner], (group, peer)) for peer in peers
    ]
    latents[inner] = latent_ref[inner]
    hidden_away[...] = hidden_ref[:, other].astype(F32)
    hidden_in_copy = copies.start(hidden_away, residual.at[core], sibling)
    residual[core] = hidden_ref[:, mine].astype(F32)
    for copy in arrivals:
        copy.wait_recv()

    stacked = latents[...].reshape(inner_count * head_count * rows, latent_width)
    for head in range(head_count):
        product = jnp.dot(stacked, value_up_ref[head], preferred_element_type=F32)
        product = product.reshape(inner_count, head_count, rows, value_width)[:, head]
        head_out[:, core, :, head * value_width : (head + 1) * value_width] = product.astype(
            BF16
        ).astype(F32)
    heads_copy = copies.start(head_out.at[:, core], head_out.at[:, core], sibling)
    load_proj.wait()
    heads_copy.wait_recv()
    heads = head_out[...].reshape(
        inner_count * CORES * rows, head_count * value_width
    ).astype(BF16)

    parts = column_parts(half, len(PLANE_ORDERS))
    scatters = []
    for (start, columns), ref, landing, order in zip(
        parts, part_refs, landing_refs, PLANE_ORDERS
    ):
        partial = jnp.dot(heads, proj[:, start : start + columns], preferred_element_type=F32)
        ref[...] = partial.astype(BF16).reshape(ref.shape)
        scatter = Scatter(copies, pos, ("x", "y"), ref, order, by_phase(landing))
        scatter.begin(0)
        scatter.send_far()
        scatter.send_near()
        scatters.append(scatter)
    for scatter in scatters:
        scatter.relay()
    for scatter in scatters:
        scatter.finish()
        scatter.begin(1)
        scatter.send_far()
        scatter.send_near()
    for scatter in scatters:
        scatter.relay()
    hidden_in_copy.wait_recv()
    square_sum = jnp.zeros((CORES * rows, 1), F32)
    for (start, columns), scatter in zip(parts, scatters):
        total = scatter.finish_last()
        total += residual[:, :, start : start + columns].reshape(CORES * rows, columns)
        attended = total.astype(BF16)
        attended_ref[:, start : start + columns] = attended
        wide = attended.astype(F32)
        square_sum += jnp.sum(wide * wide, axis=1, keepdims=True)
    squares[...] = jnp.broadcast_to(square_sum, squares.shape)
    squares_copy = copies.start(squares, squares_in, sibling)
    squares_copy.wait_recv()
    mean_square = (square_sum + squares_in[:, :1]) / model_width
    scale = lax.rsqrt(mean_square + NORM_EPS)
    normed_ref[...] = (attended_ref[...].astype(F32) * scale * gain_ref[:, mine]).astype(BF16)
    copies.finish()


def attention_call(latent, value_up, out_proj, hidden_in, gain):
    rows, model_width = hidden_in.shape
    half = model_width // CORES
    chip_rows = CORES * rows
    inner_count = latent.shape[0]
    proj_rows = out_proj.shape[0]
    parts = column_parts(half, len(PLANE_ORDERS))
    vmem = pl.BlockSpec(memory_space=pltpu.VMEM)
    hbm = pl.BlockSpec(memory_space=pl.ANY)
    copy_count = inner_count - 1 + 3 + 2 * 2 * 6
    block = jax.ShapeDtypeStruct((chip_rows, half), BF16)
    return pl.pallas_call(
        attention_kernel,
        out_shape=(block, block),
        in_specs=[vmem, vmem, hbm, vmem, vmem],
        out_specs=(vmem, vmem),
        scratch_shapes=[
            pltpu.VMEM(latent.shape, BF16),
            pltpu.VMEM((proj_rows, half), BF16),
            pltpu.VMEM((inner_count, CORES, rows, proj_rows), F32),
            pltpu.VMEM((CORES, rows, half), F32),
            pltpu.VMEM((rows, half), F32),
            pltpu.VMEM((chip_rows, LANES), F32),
            pltpu.VMEM((chip_rows, LANES), F32),
            [pltpu.VMEM((RING, RING, chip_rows, columns), BF16) for _, columns in parts],
            [landing_shapes(2, chip_rows, columns) for _, columns in parts],
            pltpu.SemaphoreType.DMA((copy_count,)),
            pltpu.SemaphoreType.DMA((copy_count,)),
            pltpu.SemaphoreType.DMA,
        ],
        compiler_params=pltpu.CompilerParams(
            collective_id=0, has_side_effects=True, vmem_limit_bytes=40 * 2**20
        ),
        name="attention_out",
    )(latent, value_up, out_proj, hidden_in, gain)


def silu(value):
    return value / (1.0 + jnp.exp(-value))


def expert_kernel(
    normed_ref,
    attended_ref,
    weight_ref,
    gate_hbm,
    up_hbm,
    down_hbm,
    shared_gate_hbm,
    shared_up_hbm,
    shared_down_hbm,
    out_ref,
    row_refs,
    inner_weights,
    shared_weights,
    down_weights,
    row_scale,
    sums,
    sums_out,
    sums_in,
    shared_sums,
    shared_in,
    hidden,
    part_refs,
    landing_refs,
    final,
    final_in,
    send_sems,
    recv_sems,
    local_sems,
):
    pos = my_position()
    core = pos["core"]
    sibling = device_at(sibling_of(pos))
    chip_rows, half = normed_ref.shape
    rows = chip_rows // CORES
    unit_count = gate_hbm.shape[2]
    shared_count = shared_gate_hbm.shape[1]
    plane_rows = RING * RING * chip_rows
    mine = pl.ds(pl.multiple_of(core * half, LANES), half)
    other = pl.ds(pl.multiple_of((1 - core) * half, LANES), half)
    parts = column_parts(half, len(GATHER_ORDERS))

    own_units = pl.ds(pl.multiple_of(core * unit_count, unit_count), unit_count)
    shared_units = pl.ds(CORES * unit_count, shared_count)
    local = [
        (gate_hbm.at[0, mine, :], inner_weights.at[2 * core]),
        (up_hbm.at[0, mine, :], inner_weights.at[2 * core + 1]),
        (shared_gate_hbm.at[mine, :], shared_weights.at[0]),
        (shared_up_hbm.at[mine, :], shared_weights.at[1]),
        (down_hbm.at[0, :, mine], down_weights.at[own_units, :]),
        (shared_down_hbm.at[:, mine], down_weights.at[shared_units, :]),
    ]
    loads = []
    for slot, (src, dst) in enumerate(local):
        load = pltpu.make_async_copy(src, dst, local_sems.at[slot])
        load.start()
        loads.append(load)
    for (start, columns), ref in zip(parts, row_refs):
        ref[pos["z"], pos["x"], pos["y"]] = normed_ref[:, start : start + columns]

    neighbours = [device_at(moved(pos, axis, by)) for axis in AXES for by in (1, -1)]
    greet(neighbours + [sibling])
    copies = Copies(send_sems, recv_sems)
    gathers = [
        Gather(copies, pos, ref, order) for ref, order in zip(row_refs, GATHER_ORDERS)
    ]
    for gather in gathers:
        gather.begin(0)
    weight_copies = [
        copies.start(gate_hbm.at[0, other, :], inner_weights.at[2 * core], sibling),
        copies.start(up_hbm.at[0, other, :], inner_weights.at[2 * core + 1], sibling),
        copies.start(down_hbm.at[0, :, other], down_weights.at[own_units, :], sibling),
    ]

    def prepare(step, carry):
        z, plane = lax.div(step, RING * RING), lax.rem(step, RING * RING)
        x, y = lax.div(plane, RING), lax.rem(plane, RING)
        for which in range(2 * CORES):
            sums[which, z, x, y] = jnp.zeros((chip_rows, unit_count), F32)
        hidden[z, x, y, :, CORES * unit_count :] = jnp.zeros((chip_rows, shared_count), BF16)
        weights = weight_ref[z, :, plane].reshape(chip_rows, weight_ref.shape[-1])
        lane = lax.broadcasted_iota(jnp.int32, weights.shape, 1)
        for which in range(CORES):
            expert = (pos["z"] * CORES + which) * RING + pos["x"]
            scale = jnp.sum(jnp.where(lane == expert, weights, 0.0), axis=1, keepdims=True)
            row_scale[which, z, x, y] = jnp.broadcast_to(scale, (chip_rows, LANES))
        return carry

    lax.fori_loop(0, RING**3, prepare, 0)

    def multiply(which_part, place):
        start, columns = parts[which_part]
        ref = row_refs[which_part]
        axis = GATHER_ORDERS[which_part][-1]
        index = view_index(AXES, {axis: place}, None, None, columns)

        def one(which, carry):
            block = ref[index].reshape(plane_rows, columns)
            product = jnp.dot(
                block,
                inner_weights[which, start : start + columns, :],
                preferred_element_type=F32,
            )
            at = (which,) + index
            sums[at] = sums[at] + product.reshape(RING, RING, chip_rows, unit_count)
            return carry

        lax.fori_loop(0, 2 * CORES, one, 0)

    for phase in range(3):
        if phase:
            for gather in gathers:
                gather.begin(phase)
        last = phase == 2
        if last:
            for load in loads:
                load.wait()
            for copy in weight_copies:
                copy.wait_recv()
            for k, gather in enumerate(gathers):
                multiply(k, pos[gather.axis])
        for gather in gathers:
            gather.relay()
        for k, gather in enumerate(gathers):
            gather.wait_near()
            if last:
                multiply(k, moved(pos, gather.axis, 1)[gather.axis])
                multiply(k, moved(pos, gather.axis, -1)[gather.axis])
        for k, gather in enumerate(gathers):
            gather.wait_far()
            if last:
                multiply(k, moved(pos, gather.axis, 2)[gather.axis])

    exchanges = []
    for z in range(RING):

        def narrow(step, carry):
            which, plane = lax.div(step, RING * RING), lax.rem(step, RING * RING)
            x, y = lax.div(plane, RING), lax.rem(plane, RING)
            sums_out[which, z, x, y] = sums[which, z, x, y].astype(BF16)
            return carry

        lax.fori_loop(0, 2 * CORES * RING * RING, narrow, 0)
        exchanges.append(copies.start(sums_out.at[:, z], sums_in.at[:, z], sibling))
    for which in range(2):
        total = jnp.zeros((plane_rows, shared_count), F32)
        for (start, columns), ref in zip(parts, row_refs):
            total += jnp.dot(
                ref[pos["z"]].reshape(plane_rows, columns),
                shared_weights[which, start : start + columns, :],
                preferred_element_type=F32,
            )
        shared_sums[which] = total
    shared_copy = copies.start(shared_sums, shared_in, sibling)
    for z in range(RING):
        exchanges[z].wait_recv()

        def activate(plane, carry):
            x, y = lax.div(plane, RING), lax.rem(plane, RING)
            for which in range(CORES):
                gate, up = (
                    sums[2 * which + k, z, x, y] + sums_in[2 * which + k, z, x, y].astype(F32)
                    for k in (0, 1)
                )
                scale = row_scale[which, z, x, y]
                scale = jnp.concatenate([scale] * (unit_count // LANES), axis=1)
                value = (silu(gate) * up * scale).astype(BF16)
                hidden[z, x, y, :, which * unit_count : (which + 1) * unit_count] = value
            return carry

        lax.fori_loop(0, RING * RING, activate, 0)
    shared_copy.wait_recv()
    shared_gate_part, shared_up_part = (shared_sums[k] + shared_in[k] for k in (0, 1))
    shared_hidden = (silu(shared_gate_part) * shared_up_part).astype(BF16)
    hidden[pos["z"], :, :, :, CORES * unit_count :] = shared_hidden.reshape(
        RING, RING, chip_rows, shared_count
    )

    scatters = [
        Scatter(copies, pos, AXES, ref, order, by_phase(landing))
        for ref, order, landing in zip(part_refs, SCATTER_ORDERS, landing_refs)
    ]

    def project(which_part, place):
        start, columns = parts[which_part]
        scatter = scatters[which_part]
        index = view_index(AXES, {scatter.axis: place}, None, None, columns)
        product = jnp.dot(
            hidden[index].reshape(plane_rows, hidden.shape[-1]),
            down_weights[:, start : start + columns],
            preferred_element_type=F32,
        )
        scatter.ref[index] = product.astype(BF16).reshape(RING, RING, chip_rows, columns)

    for k, scatter in enumerate(scatters):
        scatter.begin(0)
        project(k, scatter.across)
        scatter.send_far()
    for k, scatter in enumerate(scatters):
        project(k, scatter.above)
        project(k, scatter.below)
        scatter.send_near()
    for k, scatter in enumerate(scatters):
        project(k, pos[scatter.axis])
    for phase in range(2):
        for scatter in scatters:
            scatter.relay()
        for scatter in scatters:
            scatter.finish()
            scatter.begin(phase + 1)
            scatter.send_far()
            scatter.send_near()
    for scatter in scatters:
        scatter.relay()
    for (start, columns), scatter in zip(parts, scatters):
        total = scatter.finish_last() + attended_ref[:, start : start + columns].astype(F32)
        final[:, :, start : start + columns] = total.reshape(CORES, rows, columns)
    final_copy = copies.start(final.at[1 - core], final_in, sibling)
    out_ref[:, mine] = final[core].astype(BF16)
    final_copy.wait_recv()
    out_ref[:, other] = final_in[...].astype(BF16)
    copies.finish()


def expert_call(normed, attended, weights, gate, up, down, shared_gate, shared_up, shared_down):
    chip_rows, half = normed.shape
    rows = chip_rows // CORES
    model_width = half * CORES
    unit_count = gate.shape[2]
    shared_count = shared_gate.shape[1]
    plane_rows = RING * RING * chip_rows
    depth = CORES * unit_count + shared_count
    parts = column_parts(half, len(GATHER_ORDERS))
    vmem = pl.BlockSpec(memory_space=pltpu.VMEM)
    hbm = pl.BlockSpec(memory_space=pl.ANY)
    grid3 = (RING, RING, RING)
    copy_count = 3 * 3 * 6 * 2 + 3 + RING + 2
    return pl.pallas_call(
        expert_kernel,
        out_shape=jax.ShapeDtypeStruct((rows, model_width), BF16),
        in_specs=[vmem, vmem, vmem] + [hbm] * 6,
        out_specs=vmem,
        scratch_shapes=[
            [pltpu.VMEM(grid3 + (chip_rows, columns), BF16) for _, columns in parts],
            pltpu.VMEM((2 * CORES, half, unit_count), BF16),
            pltpu.VMEM((2, half, shared_count), BF16),
            pltpu.VMEM((depth, half), BF16),
            pltpu.VMEM((CORES,) + grid3 + (chip_rows, LANES), F32),
            pltpu.VMEM((2 * CORES,) + grid3 + (chip_rows, unit_count), F32),
            pltpu.VMEM((2 * CORES,) + grid3 + (chip_rows, unit_count), BF16),
            pltpu.VMEM((2 * CORES,) + grid3 + (chip_rows, unit_count), BF16),
            pltpu.VMEM((2, plane_rows, shared_count), F32),
            pltpu.VMEM((2, plane_rows, shared_count), F32),
            pltpu.VMEM(grid3 + (chip_rows, depth), BF16),
            [pltpu.VMEM(grid3 + (chip_rows, columns), BF16) for _, columns in parts],
            [landing_shapes(3, chip_rows, columns) for _, columns in parts],
            pltpu.VMEM((CORES, rows, half), F32),
            pltpu.VMEM((rows, half), F32),
            pltpu.SemaphoreType.DMA((copy_count,)),
            pltpu.SemaphoreType.DMA((copy_count,)),
            pltpu.SemaphoreType.DMA((6,)),
        ],
        compiler_params=pltpu.CompilerParams(
            collective_id=1, has_side_effects=True, vmem_limit_bytes=60 * 2**20
        ),
        name="experts",
    )(normed, attended, weights, gate, up, down, shared_gate, shared_up, shared_down)


def ancestors(parents):
    node_count = parents.shape[-1]
    node_ids = jnp.arange(node_count, dtype=jnp.int32)
    reach = (parents[:, :, None] == node_ids) | (node_ids[:, None] == node_ids)
    hops = 1
    while hops < node_count - 1:
        reach = jnp.any(reach[:, :, :, None] & reach[:, None, :, :], axis=2)
        hops *= 2
    return reach


def attend(queries, node_keys, cache, cache_len, visible, latent_width):
    cache_scores = (
        jnp.einsum("bnhc,blc->bnhl", queries, cache, preferred_element_type=F32) * SCALE_QK
    )
    node_scores = (
        jnp.einsum("bnhc,bmc->bnhm", queries, node_keys, preferred_element_type=F32) * SCALE_QK
    )
    positions = jnp.arange(cache.shape[1], dtype=jnp.int32)
    cache_live = positions[None, :] < cache_len[:, None]
    cache_scores = jnp.where(cache_live[:, None, None, :], cache_scores, -jnp.inf)
    node_scores = jnp.where(visible[:, :, None, :], node_scores, -jnp.inf)
    highest = jnp.maximum(jnp.max(cache_scores, axis=-1), jnp.max(node_scores, axis=-1))[..., None]
    cache_exp = jnp.exp(cache_scores - highest)
    node_exp = jnp.exp(node_scores - highest)
    exp_total = jnp.sum(cache_exp, axis=-1, keepdims=True) + jnp.sum(
        node_exp, axis=-1, keepdims=True
    )
    cache_weights = (cache_exp / exp_total).astype(BF16)
    node_weights = (node_exp / exp_total).astype(BF16)
    latent = jnp.einsum(
        "bnhl,blc->bnhc", cache_weights, cache[:, :, :latent_width], preferred_element_type=F32
    )
    latent = latent + jnp.einsum(
        "bnhm,bmc->bnhc", node_weights, node_keys[:, :, :latent_width], preferred_element_type=F32
    )
    return latent.astype(BF16)


def local(
    hidden_in,
    queries,
    node_latent,
    cache,
    cache_len,
    parents,
    value_up,
    out_proj,
    ffn_gain,
    route_experts,
    route_weights,
    expert_gate,
    expert_up,
    expert_down,
    shared_gate,
    shared_up,
    shared_down,
):
    req_count, _, query_width = cache.shape
    node_count = parents.shape[1]
    rows, head_count = queries.shape[:2]
    latent_width = value_up.shape[1]
    group_count = lax.axis_size("group")
    inner_count = lax.axis_size("ingroup")
    expert_count = group_count * RING
    named = route_experts[:, :, None] == jnp.arange(expert_count, dtype=jnp.int32)
    weights = jnp.sum(jnp.where(named, route_weights[:, :, None], 0.0), axis=1)
    weights = lax.all_gather(weights, ("group", "ingroup"), axis=0, tiled=True)
    weights = weights.reshape(group_count // CORES, CORES, inner_count, rows, expert_count)
    latent = attend(
        queries.reshape(req_count, node_count, head_count, query_width),
        node_latent.reshape(req_count, node_count, query_width),
        cache,
        cache_len,
        ancestors(parents),
        latent_width,
    )
    latent = jnp.transpose(latent.reshape(rows, head_count, latent_width), (1, 0, 2))
    latent = latent.reshape(inner_count, head_count // inner_count * rows, latent_width)
    attended, normed = attention_call(
        latent, value_up, out_proj, hidden_in, ffn_gain.reshape(1, -1)
    )
    return expert_call(
        normed,
        attended,
        weights,
        expert_gate,
        expert_up,
        expert_down,
        shared_gate,
        shared_up,
        shared_down,
    )


def solution(mesh):
    both = ("group", "ingroup")
    in_specs = (
        P(both, None),
        P(both, None, None),
        P(both, None),
        P(both, None, None),
        P(both),
        P(both, None),
        P("ingroup", None, None),
        P("ingroup", None),
        P(),
        P(both, None),
        P(both, None),
        P(both, None, None),
        P(both, None, None),
        P(both, None, None),
        P(None, "ingroup"),
        P(None, "ingroup"),
        P("ingroup", None),
    )
    return jax.shard_map(
        local, mesh=mesh, in_specs=in_specs, out_specs=P(both, None), check_vma=False
    )
```

time: 462 us -> 215 us (0.47)
  waiting for transfers between devices: 253 us -> 0 us
  Pallas kernels: 0 us -> 140 us
  blocking collectives: 113 us -> 60.2 us
  local copies, waits for them, and re-layouts: 33.9 us -> 8.75 us
  matrix products: 28.4 us -> 3.97 us
  between operations: 14.9 us -> 0.9 us
  other arithmetic: 12.8 us -> 1.05 us
  starting transfers between devices: 4.89 us -> 0 us
    unnamed x5 -> x0, waiting for transfers between devices: 162 us -> none
    pallas_call x0 -> x2, Pallas kernels: none -> 140 us  [the longest x1 101 us: expert_call(): pl.pallas_call(expert_kernel, out_shape=jax.ShapeDtypeStruct((rows, model...]
    all_to_all x2 -> x0, blocking collectives: 113 us -> none  [the longest x1 95.5 us: local(): lax.all_to_all(send_rows, ('group', 'ingroup'), split_axis=0, concat_axis...]
    all_gather x1 -> x0, waiting for transfers between devices: 90.9 us -> none  [local(): lax.all_gather(normed, 'ingroup', axis=0, tiled=True)]
    all_gather x0 -> x1, blocking collectives: none -> 60.2 us  [local(): weights = lax.all_gather(weights, ('group', 'ingroup'), axis=0, tiled=True)]
    dot_general x11 -> x2, matrix products: 27.3 us -> 2.8 us  [the longest x1 2.37 us: attend(): jnp.einsum('bnhc,blc->bnhl', queries, cache, preferred_element_type=F32)]
    convert_element_type x2 -> x1, local copies, waits for them, and re-layouts: 12.3 us -> 0.29 us  [attend(): return latent.astype(BF16)]
    reduce_sum x4 -> x1, other arithmetic: 10.3 us -> 0.09 us  [local(): weights = jnp.sum(jnp.where(named, route_weights[:, :, None], 0.0), axis=1)]
  transfers between devices with their start and end apart: 4 -> 0, of which waited for: 3 -> 0; matrix products, arithmetic and copies ran while one was open for 5% -> 0% of each run, Pallas kernels for 0% -> 0%
where the time goes in v1:
time: 215 us
  Pallas kernels  140 us (65%)
  blocking collectives  60.2 us (28%)
  local copies, waits for them, and re-layouts  8.75 us (4%)
  matrix products  3.97 us (2%)
    pallas_call x1, Pallas kernels, expert_call(): pl.pallas_call(expert_kernel, out_shape=jax.ShapeDtypeStruct((rows, model...  101 us
    all_gather x1, blocking collectives, local(): weights = lax.all_gather(weights, ('group', 'ingroup'), axis=0, tiled=True)  60.2 us
    pallas_call x1, Pallas kernels, attention_call(): pl.pallas_call(attention_kernel, out_shape=(block, block), in_specs=[vmem...  39.1 us
    unnamed x33, local copies, waits for them, and re-layouts  8.46 us

profile of v1, /device:TPU:1, one launch (start us, length us, event | category | flops | bytes accessed | tf_op | source)
XLA Modules:
  0.0 215.1 jit_solution(1954910436376091390)
XLA Ops:
  0.0 0.0 copy-start
  0.7 0.4 copy-done
  1.1 2.4 %fusion = (f32[8,64]{1,0:T(8,128)S(1)}, f32[8,64,1024]{2,1,0:T(8,128)S(1)}) fusion(pred[1024]{0:T(1024)(128)(4,1)S(1)} %iota_compare_fusion.3, bf16[8,64,576]{2,1,0:T(8,128)(2,1)S(1)} %copy-done, bf16[1,1024,576]{1,2,0:T(8,128)(2,1)} %param.20), kind=kOutput, calls=%fused_computation.3 | convolution fusion | flops 605552128 | bytes 3869696 | tf_op jit(solution)/shard_map/bnhc,blc->bnhl/dot_general | solution.py:693
  3.5 0.0 copy-start.11
  3.5 0.0 copy-done.12
  3.5 0.1 fusion.15
  3.6 0.1 and_reduce_fusion.2
  3.7 0.1 and_reduce_fusion.1
  3.8 0.1 and_reduce_fusion
  3.9 0.4 fusion.18
  4.3 0.6 fusion.1
  4.9 0.0 slice-start
  5.0 0.0 slice-start.1
  5.0 0.8 fusion.7
  5.8 0.0 copy-start.1
  5.8 0.0 copy-start.2
  5.8 0.0 copy-start.5
  5.8 0.3 fusion.3
  6.2 0.3 copy.23
  6.5 0.6 slice-done
  7.1 1.0 slice-done.1
  8.1 0.2 copy-done.1
  8.3 0.0 copy-done.5
  8.3 39.1 %attention_out.1 = (bf16[16,3584]{1,0:T(8,128)(2,1)S(1)}, bf16[16,3584]{1,0:T(8,128)(2,1)S(1)}) custom-call(bf16[16,32,512]{2,1,0:T(8,128)(2,1)S(1)} %bitcast.33, bf16[4,512,128]{2,1,0:T(8,128)(2,1)S(1)} %copy-done.1, bf16[512,7168]{1,0:T(8,128)(2,1)S(1)} %bitcast.32, bf16[8,7168]{1,0:T(8,128)(2,1)S(1)} %copy-done.2, f32[1,7168]{1,0:T(1,128)S(1)} %bitcast.34), custom_call_target="tpu_custom_call" | custom-call | tf_op jit(solution)/shard_map/attention_out/pallas_call | solution.py:381
  47.4 0.6 copy-done.3
  48.1 0.6 copy-done.4
  48.7 1.7 copy.24.shared_gate_hbm
  50.4 1.7 copy.25.shared_up_hbm
  52.1 0.1 select_reduce_fusion
  52.2 60.2 %all_gather.3 = f32[1024,32]{1,0:T(8,128)} all-gather(f32[8,32]{1,0:T(8,128)S(1)} %select_reduce_fusion), channel_id=1, replica_groups=mesh['group'=8,'ingroup'=16] {'group','ingroup'}, dimensions={0}, use_global_device_ids=true | all-gather | bytes 132096 | tf_op jit(solution)/shard_map/all_gather | solution.py:747
  112.4 101.2 %experts.1 = bf16[8,7168]{1,0:T(8,128)(2,1)} custom-call(bf16[16,3584]{1,0:T(8,128)(2,1)} %copy-done.4, bf16[16,3584]{1,0:T(8,128)(2,1)} %copy-done.3, f32[4,2,16,8,32]{4,3,2,1,0:T(8,128)} %bitcast.35, bf16[1,7168,256]{2,1,0:T(8,128)(2,1)} %gate_hbm.1, bf16[1,7168,256]{2,1,0:T(8,128)(2,1)} %up_hbm.1, bf16[1,256,7168]{2,1,0:T(8,128)(2,1)} %down_hbm.1, ...), custom_call_target="tpu_custom_call" | custom-call | tf_op jit(solution)/shard_map/experts/pallas_call | solution.py:648
  213.6 1.6 copy.29
  (20 shorter events, 0.1 us)
Async XLA Ops:
  0.0 1.1 copy-start
  1.1 2.4 %copy-start.12 = (s32[1,8]{1,0:T(1,128)S(1)}, s32[1,8]{1,0:T(1,128)}, u32[]{:S(2)}) copy-start(s32[1,8]{1,0:T(1,128)} %param.22) | copy-start | bytes 100
  1.1 2.8 %copy-start.8 = (bf16[8,576]{1,0:T(8,128)(2,1)S(1)}, bf16[8,576]{1,0:T(8,128)(2,1)}, u32[]{:S(2)}) copy-start(bf16[8,576]{1,0:T(8,128)(2,1)} %param.19) | copy-start | bytes 27652
  3.5 1.5 copy-start.11
  4.9 2.2 %slice-start = ((s8[7340032]{0:T(1024)(128)(4,1)}), s8[4194304]{0:T(1024)(128)(4,1)S(1)}, s32[]{:S(2)}) async-start(s8[7340032]{0:T(1024)(128)(4,1)} %bitcast.31), calls=%async_computation | async-start | bytes 8388608
  5.0 3.1 %slice-start.1 = ((s8[7340032]{0:T(1024)(128)(4,1)}), s8[3145728]{0:T(1024)(128)(4,1)S(1)}, s32[]{:S(2)}) async-start(s8[7340032]{0:T(1024)(128)(4,1)} %bitcast.31), calls=%async_computation.1 | async-start | bytes 6291456
  5.8 2.5 %copy-start.1 = (bf16[4,512,128]{2,1,0:T(8,128)(2,1)S(1)}, bf16[4,512,128]{2,1,0:T(8,128)(2,1)}, u32[]{:S(2)}) copy-start(bf16[4,512,128]{2,1,0:T(8,128)(2,1)} %value_up_ref.1) | copy-start | bytes 1572868
  5.8 2.5 %copy-start.2 = (bf16[8,7168]{1,0:T(8,128)(2,1)S(1)}, bf16[8,7168]{1,0:T(8,128)(2,1)}, u32[]{:S(2)}) copy-start(bf16[8,7168]{1,0:T(8,128)(2,1)} %hidden_ref.1) | copy-start | bytes 344068
  5.8 2.5 %copy-start.5 = (f32[7168]{0:T(1024)S(1)}, f32[7168]{0:T(1024)}, u32[]{:S(2)}) copy-start(f32[7168]{0:T(1024)} %param.25) | copy-start | bytes 86020
  8.3 40.4 %copy-start.6 = (bf16[7168,64]{0,1:T(8,128)(2,1)S(1)}, bf16[7168,64]{0,1:T(8,128)(2,1)}, u32[]{:S(2)}) copy-start(bf16[7168,64]{0,1:T(8,128)(2,1)} %param.31) | copy-start | bytes 2752516
  47.4 0.6 copy-start.3
  48.1 0.6 copy-start.4
  48.7 1.7 copy-start.7
  48.7 3.4 %copy-start.9 = (f32[8,8]{1,0:T(8,128)S(1)}, f32[8,8]{1,0:T(8,128)}, u32[]{:S(2)}) copy-start(f32[8,8]{1,0:T(8,128)} %param.27) | copy-start | bytes 772
  48.7 3.4 %copy-start.10 = (s32[8,8]{1,0:T(8,128)S(1)}, s32[8,8]{1,0:T(8,128)}, u32[]{:S(2)}) copy-start(s32[8,8]{1,0:T(8,128)} %param.26) | copy-start | bytes 772

commit v2 on v1

--- a/solution.py
+++ b/solution.py
@@ -15,6 +15,7 @@
 RING = 4
 CORES = 2
 LANES = 128
+VMEM_LIMIT = 62 * 2**20
 AXES = ("z", "x", "y")
 GATHER_ORDERS = (("x", "y", "z"), ("y", "z", "x"), ("z", "x", "y"))
 SCATTER_ORDERS = (("z", "x", "y"), ("x", "y", "z"), ("y", "z", "x"))
@@ -55,13 +56,6 @@
     other = dict(pos)
     other["core"] = 1 - pos["core"]
     return other
-
-
-def greet(devices):
-    barrier = pltpu.get_barrier_semaphore()
-    for device in devices:
-        pl.semaphore_signal(barrier, inc=1, device_id=device, device_id_type=MESH)
-    pl.semaphore_wait(barrier, len(devices))
 
 
 class Copies:
@@ -253,6 +247,18 @@
         block = tuple(self.pos[axis] for axis in self.axes)
         total = self.ref[block].astype(F32)
         return total + self.from_minus[...].astype(F32) + self.from_plus[...].astype(F32)
+
+
+def landing_shapes(axis_count, rows, columns):
+    shapes = []
+    for phase in range(axis_count):
+        lead = (RING,) * (axis_count - 1 - phase)
+        shapes += [pltpu.VMEM(lead + (rows, columns), BF16)] * 3
+    return shapes
+
+
+def by_phase(refs):
+    return [refs[3 * k : 3 * k + 3] for k in range(len(refs) // 3)]
 
 
 def landing_shapes(axis_count, rows, columns):
@@ -367,51 +373,64 @@
     copies.finish()
 
 
-def attention_call(latent, value_up, out_proj, hidden_in, gain):
-    rows, model_width = hidden_in.shape
-    half = model_width // CORES
-    chip_rows = CORES * rows
-    inner_count = latent.shape[0]
-    proj_rows = out_proj.shape[0]
-    parts = column_parts(half, len(PLANE_ORDERS))
-    vmem = pl.BlockSpec(memory_space=pltpu.VMEM)
-    hbm = pl.BlockSpec(memory_space=pl.ANY)
-    copy_count = inner_count - 1 + 3 + 2 * 2 * 6
-    block = jax.ShapeDtypeStruct((chip_rows, half), BF16)
-    return pl.pallas_call(
-        attention_kernel,
-        out_shape=(block, block),
-        in_specs=[vmem, vmem, hbm, vmem, vmem],
-        out_specs=(vmem, vmem),
-        scratch_shapes=[
-            pltpu.VMEM(latent.shape, BF16),
-            pltpu.VMEM((proj_rows, half), BF16),
-            pltpu.VMEM((inner_count, CORES, rows, proj_rows), F32),
-            pltpu.VMEM((CORES, rows, half), F32),
-            pltpu.VMEM((rows, half), F32),
-            pltpu.VMEM((chip_rows, LANES), F32),
-            pltpu.VMEM((chip_rows, LANES), F32),
-            [pltpu.VMEM((RING, RING, chip_rows, columns), BF16) for _, columns in parts],
-            [landing_shapes(2, chip_rows, columns) for _, columns in parts],
-            pltpu.SemaphoreType.DMA((copy_count,)),
-            pltpu.SemaphoreType.DMA((copy_count,)),
-            pltpu.SemaphoreType.DMA,
-        ],
-        compiler_params=pltpu.CompilerParams(
-            collective_id=0, has_side_effects=True, vmem_limit_bytes=40 * 2**20
-        ),
-        name="attention_out",
-    )(latent, value_up, out_proj, hidden_in, gain)
+def nt_dot(left, right):
+    return lax.dot_general(left, right, (((1,), (1,)), ((), ())), preferred_element_type=F32)
+
+
+def nn_dot(left, right):
+    return jnp.dot(left, right, preferred_element_type=F32)
 
 
 def silu(value):
     return value / (1.0 + jnp.exp(-value))
 
 
-def expert_kernel(
-    normed_ref,
-    attended_ref,
-    weight_ref,
+def visible_from(parents):
+    count = parents.shape[-1]
+    above = lax.broadcasted_iota(jnp.int32, (count, count), 0)
+    below = lax.broadcasted_iota(jnp.int32, (count, count), 1)
+    reach = ((above == parents) | (above == below)).astype(F32)
+    hops = 1
+    while hops < count - 1:
+        reach = (nn_dot(reach.astype(BF16), reach.astype(BF16)) > 0.5).astype(F32)
+        hops *= 2
+    return reach.astype(BF16)
+
+
+def routing_lanes(experts, weights, expert_count):
+    rows, top = experts.shape
+    lane = lax.rem(lax.broadcasted_iota(jnp.int32, (rows, LANES), 1), expert_count)
+    total = jnp.zeros((rows, LANES), F32)
+    for k in range(top):
+        total += jnp.where(lane == experts[:, k : k + 1], weights[:, k : k + 1], 0.0)
+    return total
+
+
+def in_three(values, expert_count):
+    high = values.astype(BF16).astype(F32)
+    middle = (values - high).astype(BF16).astype(F32)
+    low = values - high - middle
+    lane = lax.broadcasted_iota(jnp.int32, values.shape, 1)
+    terms = jnp.where(
+        lane < expert_count,
+        high,
+        jnp.where(lane < 2 * expert_count, middle, jnp.where(lane < 3 * expert_count, low, 0.0)),
+    )
+    return terms.astype(BF16)
+
+
+def layer_kernel(
+    cache_len_ref,
+    parents_ref,
+    experts_ref,
+    weights_ref,
+    hidden_ref,
+    node_ref,
+    gain_ref,
+    queries_hbm,
+    cache_hbm,
+    value_up_hbm,
+    out_proj_hbm,
     gate_hbm,
     up_hbm,
     down_hbm,
@@ -419,6 +438,20 @@
     shared_up_hbm,
     shared_down_hbm,
     out_ref,
+    queries,
+    cache,
+    value_up,
+    proj,
+    latent_out,
+    latents,
+    head_out,
+    residual,
+    hidden_away,
+    squares,
+    squares_in,
+    attended_rows,
+    plane_refs,
+    plane_landing,
     row_refs,
     inner_weights,
     shared_weights,
@@ -434,52 +467,122 @@
     landing_refs,
     final,
     final_in,
+    latent_send,
+    latent_recv,
     send_sems,
     recv_sems,
     local_sems,
 ):
     pos = my_position()
-    core = pos["core"]
+    core, group, inner = pos["core"], lax.axis_index("group"), lax.axis_index("ingroup")
     sibling = device_at(sibling_of(pos))
-    chip_rows, half = normed_ref.shape
-    rows = chip_rows // CORES
+    rows, model_width = hidden_ref.shape
+    half = model_width // CORES
+    chip_rows = CORES * rows
+    plane_rows = RING * RING * chip_rows
+    inner_count, _, latent_width = latents.shape
+    head_count, _, value_width = value_up.shape
+    all_heads, cached = queries.shape[1], cache.shape[1]
     unit_count = gate_hbm.shape[2]
-    shared_count = shared_gate_hbm.shape[1]
-    plane_rows = RING * RING * chip_rows
+    shared_count = shared_gate_hbm.shape[0]
+    expert_count = RING * CORES * RING
     mine = pl.ds(pl.multiple_of(core * half, LANES), half)
     other = pl.ds(pl.multiple_of((1 - core) * half, LANES), half)
-    parts = column_parts(half, len(GATHER_ORDERS))
-
     own_units = pl.ds(pl.multiple_of(core * unit_count, unit_count), unit_count)
     shared_units = pl.ds(CORES * unit_count, shared_count)
-    local = [
-        (gate_hbm.at[0, mine, :], inner_weights.at[2 * core]),
-        (up_hbm.at[0, mine, :], inner_weights.at[2 * core + 1]),
-        (shared_gate_hbm.at[mine, :], shared_weights.at[0]),
-        (shared_up_hbm.at[mine, :], shared_weights.at[1]),
-        (down_hbm.at[0, :, mine], down_weights.at[own_units, :]),
-        (shared_down_hbm.at[:, mine], down_weights.at[shared_units, :]),
-    ]
+
     loads = []
-    for slot, (src, dst) in enumerate(local):
-        load = pltpu.make_async_copy(src, dst, local_sems.at[slot])
-        load.start()
-        loads.append(load)
-    for (start, columns), ref in zip(parts, row_refs):
-        ref[pos["z"], pos["x"], pos["y"]] = normed_ref[:, start : start + columns]
-
-    neighbours = [device_at(moved(pos, axis, by)) for axis in AXES for by in (1, -1)]
-    greet(neighbours + [sibling])
+
+    def load(src, dst):
+        copy = pltpu.make_async_copy(src, dst, local_sems.at[len(loads)])
+        copy.start()
+        loads.append(copy)
+        return copy
+
+    first_loads = [load(queries_hbm, queries), load(cache_hbm.at[0], cache)]
+    head_loads = [load(value_up_hbm, value_up), load(out_proj_hbm.at[:, mine], proj)]
+
+    peers = [lax.rem(inner + step, inner_count) for step in range(1, inner_count)]
+    z_neighbours = [device_at(moved(pos, "z", by)) for by in (1, -1)]
+    partners = [(group, peer) for peer in peers] + z_neighbours + [sibling]
+    barrier = pltpu.get_barrier_semaphore()
+    for partner in partners:
+        pl.semaphore_signal(barrier, inc=1, device_id=partner, device_id_type=MESH)
+
+    routing = routing_lanes(experts_ref[...], weights_ref[...], expert_count)
+    hidden_away[:, :half] = hidden_ref[:, other].astype(F32)
+    hidden_away[:, half:] = routing
+    residual[core, :, :half] = hidden_ref[:, mine].astype(F32)
+    residual[core, :, half:] = routing
+
+    reach = visible_from(parents_ref[...])
+    node_keys = node_ref[...]
+    chunk_heads = all_heads // 2
+    chunk_rows = chunk_heads * rows
+    chunk_peers = inner_count // 2
+    row = lax.broadcasted_iota(jnp.int32, (chunk_rows, rows), 0)
+    lane = lax.broadcasted_iota(jnp.int32, (chunk_rows, rows), 1)
+    node_of = (lax.div(row, chunk_heads) == lane).astype(F32).astype(BF16)
+    seen = nt_dot(node_of, reach) > 0.5
+    to_row = lax.broadcasted_iota(jnp.int32, (chunk_rows, chunk_rows), 0)
+    from_row = lax.broadcasted_iota(jnp.int32, (chunk_rows, chunk_rows), 1)
+    head_major = (
+        (from_row == lax.rem(to_row, rows) * chunk_heads + lax.div(to_row, rows))
+        .astype(F32)
+        .astype(BF16)
+    )
+    for copy in first_loads:
+        copy.wait()
+
+    def latent_copy(peer):
+        return pltpu.make_async_remote_copy(
+            src_ref=latent_out.at[peer],
+            dst_ref=latents.at[inner],
+            send_sem=latent_send.at[peer],
+            recv_sem=latent_recv.at[inner],
+            device_id=(group, peer),
+            device_id_type=MESH,
+        )
+
+    for chunk in range(2):
+        query = queries[:, chunk * chunk_heads : (chunk + 1) * chunk_heads, :]
+        query = query.reshape(chunk_rows, query.shape[-1])
+        scores = nn_dot(query, cache[...]) * SCALE_QK
+        live = lax.broadcasted_iota(jnp.int32, scores.shape, 1) < cache_len_ref[0]
+        scores = jnp.where(live, scores, -jnp.inf)
+        node_scores = jnp.where(seen, nt_dot(query, node_keys) * SCALE_QK, -jnp.inf)
+        highest = jnp.maximum(
+            jnp.max(scores, axis=1, keepdims=True), jnp.max(node_scores, axis=1, keepdims=True)
+        )
+        scores = jnp.exp(scores - highest)
+        node_scores = jnp.exp(node_scores - highest)
+        total = jnp.sum(scores, axis=1, keepdims=True) + jnp.sum(
+            node_scores, axis=1, keepdims=True
+        )
+        share = 1.0 / total
+        latent = nt_dot((scores * share).astype(BF16), cache[:latent_width, :])
+        latent += nn_dot((node_scores * share).astype(BF16), node_keys[:, :latent_width])
+        latent = nn_dot(head_major, latent.astype(BF16)).astype(BF16)
+        latent_out[chunk * chunk_peers : (chunk + 1) * chunk_peers] = latent.reshape(
+            chunk_peers, head_count * rows, latent_width
+        )
+        if chunk == 0:
+            pl.semaphore_wait(barrier, len(partners))
+        for peer in range(chunk * chunk_peers, (chunk + 1) * chunk_peers):
+
+            @pl.when(inner != peer)
+            def _(peer=peer):
+                latent_copy(peer).start()
+
     copies = Copies(send_sems, recv_sems)
-    gathers = [
-        Gather(copies, pos, ref, order) for ref, order in zip(row_refs, GATHER_ORDERS)
-    ]
-    for gather in gathers:
-        gather.begin(0)
-    weight_copies = [
-        copies.start(gate_hbm.at[0, other, :], inner_weights.at[2 * core], sibling),
-        copies.start(up_hbm.at[0, other, :], inner_weights.at[2 * core + 1], sibling),
-        copies.start(down_hbm.at[0, :, other], down_weights.at[own_units, :], sibling),
+    hidden_copy = copies.start(hidden_away, residual.at[core], sibling)
+    late_loads = [
+        load(gate_hbm.at[0, mine, :], inner_weights.at[2 * core]),
+        load(up_hbm.at[0, mine, :], inner_weights.at[2 * core + 1]),
+        load(shared_gate_hbm.at[:, mine], shared_weights.at[0]),
+        load(shared_up_hbm.at[:, mine], shared_weights.at[1]),
+        load(down_hbm.at[0, :, mine], down_weights.at[own_units, :]),
+        load(shared_down_hbm.at[:, mine], down_weights.at[shared_units, :]),
     ]
 
     def prepare(step, carry):
@@ -488,15 +591,89 @@
         for which in range(2 * CORES):
             sums[which, z, x, y] = jnp.zeros((chip_rows, unit_count), F32)
         hidden[z, x, y, :, CORES * unit_count :] = jnp.zeros((chip_rows, shared_count), BF16)
-        weights = weight_ref[z, :, plane].reshape(chip_rows, weight_ref.shape[-1])
-        lane = lax.broadcasted_iota(jnp.int32, weights.shape, 1)
-        for which in range(CORES):
-            expert = (pos["z"] * CORES + which) * RING + pos["x"]
-            scale = jnp.sum(jnp.where(lane == expert, weights, 0.0), axis=1, keepdims=True)
-            row_scale[which, z, x, y] = jnp.broadcast_to(scale, (chip_rows, LANES))
         return carry
 
     lax.fori_loop(0, RING**3, prepare, 0)
+
+    latents[inner] = latent_out[inner]
+    for peer in range(inner_count):
+
+        @pl.when(inner != peer)
+        def _(peer=peer):
+            pltpu.make_async_remote_copy(
+                src_ref=latent_out.at[peer],
+                dst_ref=latents.at[peer],
+                send_sem=latent_send.at[peer],
+                recv_sem=latent_recv.at[peer],
+                device_id=(group, peer),
+                device_id_type=MESH,
+            ).wait_recv()
+
+    for copy in head_loads:
+        copy.wait()
+    stacked = latents[...].reshape(inner_count * head_count * rows, latent_width)
+    for head in range(head_count):
+        product = nn_dot(stacked, value_up[head])
+        product = product.reshape(inner_count, head_count, rows, value_width)[:, head]
+        head_out[:, core, :, head * value_width : (head + 1) * value_width] = product.astype(
+            BF16
+        ).astype(F32)
+    heads_copy = copies.start(head_out.at[:, core], head_out.at[:, core], sibling)
+    heads_copy.wait_recv()
+    weight_copies = [
+        copies.start(gate_hbm.at[0, other, :], inner_weights.at[2 * core], sibling),
+        copies.start(up_hbm.at[0, other, :], inner_weights.at[2 * core + 1], sibling),
+        copies.start(down_hbm.at[0, :, other], down_weights.at[own_units, :], sibling),
+    ]
+    heads = head_out[...].reshape(plane_rows, head_count * value_width).astype(BF16)
+
+    plane_parts = column_parts(half, len(PLANE_ORDERS))
+    scatters = []
+    for (start, columns), ref, landing, order in zip(
+        plane_parts, plane_refs, plane_landing, PLANE_ORDERS
+    ):
+        partial = nn_dot(heads, proj[:, start : start + columns])
+        ref[...] = partial.astype(BF16).reshape(ref.shape)
+        scatter = Scatter(copies, pos, ("x", "y"), ref, order, by_phase(landing))
+        scatter.begin(0)
+        scatter.send_far()
+        scatter.send_near()
+        scatters.append(scatter)
+    for scatter in scatters:
+        scatter.relay()
+    for scatter in scatters:
+        scatter.finish()
+        scatter.begin(1)
+        scatter.send_far()
+        scatter.send_near()
+    for scatter in scatters:
+        scatter.relay()
+    hidden_copy.wait_recv()
+    square_sum = jnp.zeros((chip_rows, 1), F32)
+    for (start, columns), scatter in zip(plane_parts, scatters):
+        total = scatter.finish_last()
+        total += residual[:, :, start : start + columns].reshape(chip_rows, columns)
+        attended = total.astype(BF16)
+        attended_rows[:, start : start + columns] = attended
+        wide = attended.astype(F32)
+        square_sum += jnp.sum(wide * wide, axis=1, keepdims=True)
+    squares[...] = jnp.broadcast_to(square_sum, squares.shape)
+    squares_copy = copies.start(squares, squares_in, sibling)
+    squares_copy.wait_recv()
+    mean_square = (square_sum + squares_in[:, :1]) / model_width
+    scale = lax.rsqrt(mean_square + NORM_EPS)
+    normed = (attended_rows[...].astype(F32) * scale * gain_ref[:, mine]).astype(BF16)
+
+    parts = column_parts(half, len(GATHER_ORDERS))
+    for (start, columns), ref in zip(parts, row_refs):
+        ref[pos["z"], pos["x"], pos["y"], :, :columns] = normed[:, start : start + columns]
+    weighed = parts[1][1]
+    row_refs[1][pos["z"], pos["x"], pos["y"], :, weighed:] = in_three(
+        residual[:, :, half:].reshape(chip_rows, LANES), expert_count
+    )
+    gathers = [
+        Gather(copies, pos, ref, order) for ref, order in zip(row_refs, GATHER_ORDERS)
+    ]
 
     def multiply(which_part, place):
         start, columns = parts[which_part]
@@ -505,12 +682,8 @@
         index = view_index(AXES, {axis: place}, None, None, columns)
 
         def one(which, carry):
-            block = ref[index].reshape(plane_rows, columns)
-            product = jnp.dot(
-                block,
-                inner_weights[which, start : start + columns, :],
-                preferred_element_type=F32,
-            )
+            block = ref[index[:-1] + (slice(0, columns),)].reshape(plane_rows, columns)
+            product = nn_dot(block, inner_weights[which, start : start + columns, :])
             at = (which,) + index
             sums[at] = sums[at] + product.reshape(RING, RING, chip_rows, unit_count)
             return carry
@@ -518,13 +691,12 @@
         lax.fori_loop(0, 2 * CORES, one, 0)
 
     for phase in range(3):
-        if phase:
-            for gather in gathers:
-                gather.begin(phase)
+        for gather in gathers:
+            gather.begin(phase)
         last = phase == 2
         if last:
-            for load in loads:
-                load.wait()
+            for copy in late_loads:
+                copy.wait()
             for copy in weight_copies:
                 copy.wait_recv()
             for k, gather in enumerate(gathers):
@@ -555,13 +727,19 @@
     for which in range(2):
         total = jnp.zeros((plane_rows, shared_count), F32)
         for (start, columns), ref in zip(parts, row_refs):
-            total += jnp.dot(
-                ref[pos["z"]].reshape(plane_rows, columns),
-                shared_weights[which, start : start + columns, :],
-                preferred_element_type=F32,
+            total += nt_dot(
+                ref[pos["z"], :, :, :, :columns].reshape(plane_rows, columns),
+                shared_weights[which, :, start : start + columns],
             )
         shared_sums[which] = total
     shared_copy = copies.start(shared_sums, shared_in, sibling)
+    picks_from = lax.broadcasted_iota(jnp.int32, (LANES, CORES * LANES), 0)
+    picks_to = lax.div(lax.broadcasted_iota(jnp.int32, (LANES, CORES * LANES), 1), LANES)
+    chosen = (pos["z"] * CORES + picks_to) * RING + pos["x"]
+    picks = ((lax.rem(picks_from, expert_count) == chosen).astype(F32)).astype(BF16)
+    for z in range(RING):
+        terms = row_refs[1][z, :, :, :, weighed:].reshape(plane_rows, LANES)
+        row_scale[z] = nn_dot(terms, picks).reshape(RING, RING, chip_rows, CORES * LANES)
     for z in range(RING):
         exchanges[z].wait_recv()
 
@@ -572,7 +750,7 @@
                     sums[2 * which + k, z, x, y] + sums_in[2 * which + k, z, x, y].astype(F32)
                     for k in (0, 1)
                 )
-                scale = row_scale[which, z, x, y]
+                scale = row_scale[z, x, y, :, which * LANES : (which + 1) * LANES]
                 scale = jnp.concatenate([scale] * (unit_count // LANES), axis=1)
                 value = (silu(gate) * up * scale).astype(BF16)
                 hidden[z, x, y, :, which * unit_count : (which + 1) * unit_count] = value
@@ -595,10 +773,9 @@
         start, columns = parts[which_part]
         scatter = scatters[which_part]
         index = view_index(AXES, {scatter.axis: place}, None, None, columns)
-        product = jnp.dot(
+        product = nn_dot(
             hidden[index].reshape(plane_rows, hidden.shape[-1]),
             down_weights[:, start : start + columns],
-            preferred_element_type=F32,
         )
         scatter.ref[index] = product.astype(BF16).reshape(RING, RING, chip_rows, columns)
 
@@ -623,97 +800,18 @@
     for scatter in scatters:
         scatter.relay()
     for (start, columns), scatter in zip(parts, scatters):
-        total = scatter.finish_last() + attended_ref[:, start : start + columns].astype(F32)
+        total = scatter.finish_last() + attended_rows[:, start : start + columns].astype(F32)
         final[:, :, start : start + columns] = total.reshape(CORES, rows, columns)
     final_copy = copies.start(final.at[1 - core], final_in, sibling)
     out_ref[:, mine] = final[core].astype(BF16)
     final_copy.wait_recv()
     out_ref[:, other] = final_in[...].astype(BF16)
     copies.finish()
-
-
-def expert_call(normed, attended, weights, gate, up, down, shared_gate, shared_up, shared_down):
-    chip_rows, half = normed.shape
-    rows = chip_rows // CORES
-    model_width = half * CORES
-    unit_count = gate.shape[2]
-    shared_count = shared_gate.shape[1]
-    plane_rows = RING * RING * chip_rows
-    depth = CORES * unit_count + shared_count
-    parts = column_parts(half, len(GATHER_ORDERS))
-    vmem = pl.BlockSpec(memory_space=pltpu.VMEM)
-    hbm = pl.BlockSpec(memory_space=pl.ANY)
-    grid3 = (RING, RING, RING)
-    copy_count = 3 * 3 * 6 * 2 + 3 + RING + 2
-    return pl.pallas_call(
-        expert_kernel,
-        out_shape=jax.ShapeDtypeStruct((rows, model_width), BF16),
-        in_specs=[vmem, vmem, vmem] + [hbm] * 6,
-        out_specs=vmem,
-        scratch_shapes=[
-            [pltpu.VMEM(grid3 + (chip_rows, columns), BF16) for _, columns in parts],
-            pltpu.VMEM((2 * CORES, half, unit_count), BF16),
-            pltpu.VMEM((2, half, shared_count), BF16),
-            pltpu.VMEM((depth, half), BF16),
-            pltpu.VMEM((CORES,) + grid3 + (chip_rows, LANES), F32),
-            pltpu.VMEM((2 * CORES,) + grid3 + (chip_rows, unit_count), F32),
-            pltpu.VMEM((2 * CORES,) + grid3 + (chip_rows, unit_count), BF16),
-            pltpu.VMEM((2 * CORES,) + grid3 + (chip_rows, unit_count), BF16),
-            pltpu.VMEM((2, plane_rows, shared_count), F32),
-            pltpu.VMEM((2, plane_rows, shared_count), F32),
-            pltpu.VMEM(grid3 + (chip_rows, depth), BF16),
-            [pltpu.VMEM(grid3 + (chip_rows, columns), BF16) for _, columns in parts],
-            [landing_shapes(3, chip_rows, columns) for _, columns in parts],
-            pltpu.VMEM((CORES, rows, half), F32),
-            pltpu.VMEM((rows, half), F32),
-            pltpu.SemaphoreType.DMA((copy_count,)),
-            pltpu.SemaphoreType.DMA((copy_count,)),
-            pltpu.SemaphoreType.DMA((6,)),
-        ],
-        compiler_params=pltpu.CompilerParams(
-            collective_id=1, has_side_effects=True, vmem_limit_bytes=60 * 2**20
-        ),
-        name="experts",
-    )(normed, attended, weights, gate, up, down, shared_gate, shared_up, shared_down)
-
-
-def ancestors(parents):
-    node_count = parents.shape[-1]
-    node_ids = jnp.arange(node_count, dtype=jnp.int32)
-    reach = (parents[:, :, None] == node_ids) | (node_ids[:, None] == node_ids)
-    hops = 1
-    while hops < node_count - 1:
-        reach = jnp.any(reach[:, :, :, None] & reach[:, None, :, :], axis=2)
-        hops *= 2
-    return reach
-
-
-def attend(queries, node_keys, cache, cache_len, visible, latent_width):
-    cache_scores = (
-        jnp.einsum("bnhc,blc->bnhl", queries, cache, preferred_element_type=F32) * SCALE_QK
-    )
-    node_scores = (
-        jnp.einsum("bnhc,bmc->bnhm", queries, node_keys, preferred_element_type=F32) * SCALE_QK
-    )
-    positions = jnp.arange(cache.shape[1], dtype=jnp.int32)
-    cache_live = positions[None, :] < cache_len[:, None]
-    cache_scores = jnp.where(cache_live[:, None, None, :], cache_scores, -jnp.inf)
-    node_scores = jnp.where(visible[:, :, None, :], node_scores, -jnp.inf)
-    highest = jnp.maximum(jnp.max(cache_scores, axis=-1), jnp.max(node_scores, axis=-1))[..., None]
-    cache_exp = jnp.exp(cache_scores - highest)
-    node_exp = jnp.exp(node_scores - highest)
-    exp_total = jnp.sum(cache_exp, axis=-1, keepdims=True) + jnp.sum(
-        node_exp, axis=-1, keepdims=True
-    )
-    cache_weights = (cache_exp / exp_total).astype(BF16)
-    node_weights = (node_exp / exp_total).astype(BF16)
-    latent = jnp.einsum(
-        "bnhl,blc->bnhc", cache_weights, cache[:, :, :latent_width], preferred_element_type=F32
-    )
-    latent = latent + jnp.einsum(
-        "bnhm,bmc->bnhc", node_weights, node_keys[:, :, :latent_width], preferred_element_type=F32
-    )
-    return latent.astype(BF16)
+    for peer in range(inner_count):
+
+        @pl.when(inner != peer)
+        def _(peer=peer):
+            latent_copy(peer).wait_send()
 
 
 def local(
@@ -735,39 +833,87 @@
     shared_up,
     shared_down,
 ):
-    req_count, _, query_width = cache.shape
-    node_count = parents.shape[1]
-    rows, head_count = queries.shape[:2]
-    latent_width = value_up.shape[1]
-    group_count = lax.axis_size("group")
+    rows, model_width = hidden_in.shape
+    half = model_width // CORES
+    chip_rows = CORES * rows
     inner_count = lax.axis_size("ingroup")
-    expert_count = group_count * RING
-    named = route_experts[:, :, None] == jnp.arange(expert_count, dtype=jnp.int32)
-    weights = jnp.sum(jnp.where(named, route_weights[:, :, None], 0.0), axis=1)
-    weights = lax.all_gather(weights, ("group", "ingroup"), axis=0, tiled=True)
-    weights = weights.reshape(group_count // CORES, CORES, inner_count, rows, expert_count)
-    latent = attend(
-        queries.reshape(req_count, node_count, head_count, query_width),
-        node_latent.reshape(req_count, node_count, query_width),
-        cache,
+    head_count, latent_width, value_width = value_up.shape
+    proj_rows = out_proj.shape[0]
+    unit_count = expert_gate.shape[2]
+    shared_count = shared_gate.shape[1]
+    plane_rows = RING * RING * chip_rows
+    depth = CORES * unit_count + shared_count
+    plane_parts = column_parts(half, len(PLANE_ORDERS))
+    parts = column_parts(half, len(GATHER_ORDERS))
+    gathered = [columns + (LANES if k == 1 else 0) for k, (_, columns) in enumerate(parts)]
+    grid3 = (RING, RING, RING)
+    vmem = pl.BlockSpec(memory_space=pltpu.VMEM)
+    smem = pl.BlockSpec(memory_space=pltpu.SMEM)
+    hbm = pl.BlockSpec(memory_space=pl.ANY)
+    copy_count = 2 * 2 * 6 + 3 * 3 * 6 * 2 + 3 + RING + 5
+    load_count = 10
+    return pl.pallas_call(
+        layer_kernel,
+        out_shape=jax.ShapeDtypeStruct((rows, model_width), BF16),
+        in_specs=[smem] + [vmem] * 6 + [hbm] * 10,
+        out_specs=vmem,
+        scratch_shapes=[
+            pltpu.VMEM(queries.shape, BF16),
+            pltpu.VMEM((cache.shape[2], cache.shape[1]), BF16),
+            pltpu.VMEM(value_up.shape, BF16),
+            pltpu.VMEM((proj_rows, half), BF16),
+            pltpu.VMEM((inner_count, head_count * rows, latent_width), BF16),
+            pltpu.VMEM((inner_count, head_count * rows, latent_width), BF16),
+            pltpu.VMEM((inner_count, CORES, rows, proj_rows), F32),
+            pltpu.VMEM((CORES, rows, half + LANES), F32),
+            pltpu.VMEM((rows, half + LANES), F32),
+            pltpu.VMEM((chip_rows, LANES), F32),
+            pltpu.VMEM((chip_rows, LANES), F32),
+            pltpu.VMEM((chip_rows, half), BF16),
+            [pltpu.VMEM((RING, RING, chip_rows, columns), BF16) for _, columns in plane_parts],
+            [landing_shapes(2, chip_rows, columns) for _, columns in plane_parts],
+            [pltpu.VMEM(grid3 + (chip_rows, columns), BF16) for columns in gathered],
+            pltpu.VMEM((2 * CORES, half, unit_count), BF16),
+            pltpu.VMEM((2, shared_count, half), BF16),
+            pltpu.VMEM((depth, half), BF16),
+            pltpu.VMEM(grid3 + (chip_rows, CORES * LANES), F32),
+            pltpu.VMEM((2 * CORES,) + grid3 + (chip_rows, unit_count), F32),
+            pltpu.VMEM((2 * CORES,) + grid3 + (chip_rows, unit_count), BF16),
+            pltpu.VMEM((2 * CORES,) + grid3 + (chip_rows, unit_count), BF16),
+            pltpu.VMEM((2, plane_rows, shared_count), F32),
+            pltpu.VMEM((2, plane_rows, shared_count), F32),
+            pltpu.VMEM(grid3 + (chip_rows, depth), BF16),
+            [pltpu.VMEM(grid3 + (chip_rows, columns), BF16) for _, columns in parts],
+            [landing_shapes(3, chip_rows, columns) for _, columns in parts],
+            pltpu.VMEM((CORES, rows, half), F32),
+            pltpu.VMEM((rows, half), F32),
+            pltpu.SemaphoreType.DMA((inner_count,)),
+            pltpu.SemaphoreType.DMA((inner_count,)),
+            pltpu.SemaphoreType.DMA((copy_count,)),
+            pltpu.SemaphoreType.DMA((copy_count,)),
+            pltpu.SemaphoreType.DMA((load_count,)),
+        ],
+        compiler_params=pltpu.CompilerParams(
+            collective_id=0, has_side_effects=True, vmem_limit_bytes=VMEM_LIMIT
+        ),
+        name="layer",
+    )(
         cache_len,
-        ancestors(parents),
-        latent_width,
-    )
-    latent = jnp.transpose(latent.reshape(rows, head_count, latent_width), (1, 0, 2))
-    latent = latent.reshape(inner_count, head_count // inner_count * rows, latent_width)
-    attended, normed = attention_call(
-        latent, value_up, out_proj, hidden_in, ffn_gain.reshape(1, -1)
-    )
-    return expert_call(
-        normed,
-        attended,
-        weights,
+        parents,
+        route_experts,
+        route_weights,
+        hidden_in,
+        node_latent,
+        ffn_gain.reshape(1, -1),
+        queries,
+        jnp.swapaxes(cache, 1, 2),
+        value_up,
+        out_proj,
         expert_gate,
         expert_up,
         expert_down,
-        shared_gate,
-        shared_up,
+        jnp.swapaxes(shared_gate, 0, 1),
+        jnp.swapaxes(shared_up, 0, 1),
         shared_down,
     )
 

time: 215 us -> 140 us (0.65)
  blocking collectives: 60.2 us -> 0 us
  local copies, waits for them, and re-layouts: 8.75 us -> 1.55 us
  matrix products: 3.97 us -> 0 us
    all_gather x1 -> x0, blocking collectives: 60.2 us -> none  [local(): weights = lax.all_gather(weights, ('group', 'ingroup'), axis=0, tiled=True)]
    unnamed x33 -> x1, local copies, waits for them, and re-layouts: 8.46 us -> 1.55 us
    dot_general x4 -> x0, matrix products: 3.97 us -> none  [the longest x1 2.37 us: attend(): jnp.einsum('bnhc,blc->bnhl', queries, cache, preferred_element_type=F32)]
    pallas_call x2 -> x1, Pallas kernels: 140 us -> 138 us  [local(): pl.pallas_call(layer_kernel, out_shape=jax.ShapeDtypeStruct((rows, model_...]
where the time goes in v2:
time: 140 us
  Pallas kernels  138 us (99%)
  local copies, waits for them, and re-layouts  1.55 us (1%)
    pallas_call x1, Pallas kernels, local(): pl.pallas_call(layer_kernel, out_shape=jax.ShapeDtypeStruct((rows, model_...  138 us

profile of v2, /device:TPU:1, one launch (start us, length us, event | category | flops | bytes accessed | tf_op | source)
XLA Modules:
  0.0 140.3 jit_solution(8417710848096589580)
XLA Ops:
  0.7 138.1 %layer.1 = bf16[8,7168]{1,0:T(8,128)(2,1)} custom-call(s32[1]{0:T(128)S(6)} %copy.19.cache_len_ref, s32[1,8]{1,0:T(1,128)} %parents_ref.1, s32[8,8]{1,0:T(8,128)} %experts_ref.1, f32[8,8]{1,0:T(8,128)} %weights_ref.1, bf16[8,7168]{1,0:T(8,128)(2,1)} %hidden_ref.1, bf16[8,576]{1,0:T(8,128)(2,1)} %node_ref.1, f32[1,7168]{1,0:T(1,128)} %bitcast.7, ...), custom_call_target="tpu_custom_call" | custom-call | tf_op jit(solution)/shard_map/layer/pallas_call | solution.py:855
  138.7 1.6 %copy.20 = bf16[8,7168]{1,0:T(8,128)(2,1)} copy(bf16[8,7168]{1,0:T(8,128)(2,1)} %layer.1) | data formatting | bytes 229376

commit v3 on v2

--- a/solution.py
+++ b/solution.py
@@ -81,15 +81,23 @@
             copy.wait_send()
 
 
-def view_index(axes, fixed, split_axis, half, columns):
+OFFSETS = (0, 1, -1, 2)
+FACING = (0, 2, 1, 3)
+NEXT, BEFORE, FAR = 1, 2, 3
+WHOLE, OTHERS = (0, RING), (1, RING - 1)
+
+
+def view_index(axes, chosen, split_axis, half, columns):
     index = []
     for axis in axes:
-        if axis in fixed:
-            index.append(fixed[axis])
-        elif axis == split_axis and half is not None:
-            index.append(pl.ds(half * (RING // 2), RING // 2))
+        at = chosen[axis]
+        if isinstance(at, tuple):
+            start, size = at
+            if axis == split_axis and half is not None:
+                start, size = start + half * (size // 2), size // 2
+            index.append(pl.ds(start, size))
         else:
-            index.append(slice(None))
+            index.append(at)
     index.append(slice(None))
     if split_axis is None and half is not None:
         low = (columns // LANES + 1) // 2 * LANES
@@ -99,38 +107,64 @@
     return tuple(index)
 
 
-class Gather:
-    def __init__(self, copies, pos, ref, order):
-        self.copies, self.pos, self.ref, self.order = copies, pos, ref, order
+def over_blocks(axes, chosen, split_axis, half, body):
+    spans = []
+    for axis in axes:
+        at = chosen[axis]
+        start, size = at if isinstance(at, tuple) else (at, 1)
+        if axis == split_axis and half is not None:
+            start, size = start + half * (size // 2), size // 2
+        spans.append((axis, start, size))
+    steps = 1
+    for _, _, size in spans:
+        steps *= size
+
+    def one(step, carry):
+        places, rest = {}, step
+        for axis, start, size in reversed(spans):
+            if size == 1:
+                places[axis] = start
+            else:
+                places[axis] = start + lax.rem(rest, size)
+                rest = lax.div(rest, size)
+        body(places)
+        return carry
+
+    if steps == 1:
+        one(0, 0)
+    else:
+        lax.fori_loop(0, steps, one, 0)
+
+
+class Ring:
+    def __init__(self, copies, pos, ref, axes, axis, chosen, split_axis):
+        self.copies, self.ref, self.axes, self.axis = copies, ref, axes, axis
+        self.chosen, self.split_axis = chosen, split_axis
         self.columns = ref.shape[-1]
-
-    def view(self, place, half):
-        fixed = {axis: self.pos[axis] for axis in self.order[self.phase + 1 :]}
-        fixed[self.axis] = place
-        split_axis = self.order[0] if self.phase else None
-        return self.ref.at[view_index(AXES, fixed, split_axis, half, self.columns)]
-
-    def begin(self, phase):
-        self.phase, self.axis = phase, self.order[phase]
-        pos, axis = self.pos, self.axis
         self.plus, self.minus = device_at(moved(pos, axis, 1)), device_at(moved(pos, axis, -1))
-        own = [self.view(pos[axis], half) for half in (0, 1)]
+
+    def block(self, place, half):
+        chosen = dict(self.chosen)
+        chosen[self.axis] = place
+        return self.ref.at[view_index(self.axes, chosen, self.split_axis, half, self.columns)]
+
+
+class Gather(Ring):
+    def begin(self):
+        start, block = self.copies.start, self.block
         self.first = [
-            self.copies.start(own[0], own[0], self.plus),
-            self.copies.start(own[1], own[1], self.minus),
-            self.copies.start(own[1], own[1], self.plus),
-            self.copies.start(own[0], own[0], self.minus),
+            start(block(0, 0), block(BEFORE, 0), self.plus),
+            start(block(0, 1), block(NEXT, 1), self.minus),
+            start(block(0, 1), block(BEFORE, 1), self.plus),
+            start(block(0, 0), block(NEXT, 0), self.minus),
         ]
 
     def relay(self):
-        below = moved(self.pos, self.axis, -1)[self.axis]
-        above = moved(self.pos, self.axis, 1)[self.axis]
+        start, block = self.copies.start, self.block
         self.first[0].wait_recv()
-        low = self.view(below, 0)
-        self.far = [self.copies.start(low, low, self.plus)]
+        self.far = [start(block(BEFORE, 0), block(FAR, 0), self.plus)]
         self.first[1].wait_recv()
-        high = self.view(above, 1)
-        self.far.append(self.copies.start(high, high, self.minus))
+        self.far.append(start(block(NEXT, 1), block(FAR, 1), self.minus))
 
     def wait_near(self):
         self.first[2].wait_recv()
@@ -141,98 +175,56 @@
         self.far[1].wait_recv()
 
 
-class Scatter:
-    def __init__(self, copies, pos, axes, ref, order, landing):
-        self.copies, self.pos, self.axes, self.ref = copies, pos, axes, ref
-        self.order, self.landing = order, landing
-        self.columns = ref.shape[-1]
-
-    def begin(self, phase):
-        self.phase, self.axis = phase, self.order[phase]
-        self.later = tuple(axis for axis in self.axes if axis in self.order[phase + 1 :])
-        self.split_axis = self.order[-1] if self.later else None
-        self.relayed, self.from_minus, self.from_plus = self.landing[phase]
-        pos, axis = self.pos, self.axis
-        self.above, self.below = moved(pos, axis, 1)[axis], moved(pos, axis, -1)[axis]
-        self.across = moved(pos, axis, 2)[axis]
-        self.plus, self.minus = device_at(moved(pos, axis, 1)), device_at(moved(pos, axis, -1))
-
-    def fixed(self, place):
-        fixed = {axis: self.pos[axis] for axis in self.order[: self.phase]}
-        fixed[self.axis] = place
-        return fixed
-
-    def block(self, place, half):
-        return self.ref.at[
-            view_index(self.axes, self.fixed(place), self.split_axis, half, self.columns)
+class Scatter(Ring):
+    def land(self, landing):
+        self.later = tuple(a for a in self.axes if isinstance(self.chosen.get(a), tuple))
+        self.landing_axes, self.landing = landing
+        self.relayed, self.from_before, self.from_next = self.landing
+        return self
+
+    def landed(self, ref, half):
+        return ref.at[
+            view_index(self.landing_axes, self.chosen, self.split_axis, half, self.columns)
         ]
-
-    def landed(self, ref, half):
-        return ref.at[view_index(self.later, {}, self.split_axis, half, self.columns)]
 
     def send_far(self):
         start = self.copies.start
         self.far = [
-            start(self.block(self.across, 0), self.landed(self.relayed, 0), self.plus),
-            start(self.block(self.across, 1), self.landed(self.relayed, 1), self.minus),
+            start(self.block(FAR, 0), self.landed(self.relayed, 0), self.plus),
+            start(self.block(FAR, 1), self.landed(self.relayed, 1), self.minus),
         ]
 
     def send_near(self):
         start = self.copies.start
         self.near = [
-            start(self.block(self.above, 1), self.landed(self.from_minus, 1), self.plus),
-            start(self.block(self.below, 0), self.landed(self.from_plus, 0), self.minus),
+            start(self.block(NEXT, 1), self.landed(self.from_before, 1), self.plus),
+            start(self.block(BEFORE, 0), self.landed(self.from_next, 0), self.minus),
         ]
 
     def add_into(self, place, half, refs):
-        if not self.later:
-            block = view_index(self.axes, self.fixed(place), None, half, self.columns)
-            land = view_index((), {}, None, half, self.columns)
+        tail = view_index((), {}, self.split_axis, half, self.columns)
+
+        def slab(places):
+            both = dict(self.chosen)
+            both.update(places)
+            both[self.axis] = place
+            block = tuple(both[axis] for axis in self.axes) + tail
+            land = tuple(both[axis] for axis in self.landing_axes) + tail
             total = self.ref[block].astype(F32)
             for ref in refs:
                 total += ref[land].astype(F32)
             self.ref[block] = total.astype(BF16)
-            return
-        spans = [
-            RING // 2 if axis == self.split_axis and half is not None else RING
-            for axis in self.later
-        ]
-        steps = 1
-        for span in spans:
-            steps *= span
-
-        def slab(step, carry):
-            places, rest = {}, step
-            for axis, span in reversed(list(zip(self.later, spans))):
-                place_in = lax.rem(rest, span)
-                rest = lax.div(rest, span)
-                if axis == self.split_axis and half is not None:
-                    place_in = place_in + half * (RING // 2)
-                places[axis] = place_in
-            land = tuple(places[axis] for axis in self.later)
-            both = dict(places)
-            both.update(self.fixed(place))
-            block = tuple(both[axis] for axis in self.axes)
-            total = self.ref[block].astype(F32)
-            for ref in refs:
-                total += ref[land].astype(F32)
-            self.ref[block] = total.astype(BF16)
-            return carry
-
-        lax.fori_loop(0, steps, slab, 0)
+
+        over_blocks(self.later, self.chosen, self.split_axis, half, slab)
 
     def relay(self):
         start = self.copies.start
         self.far[0].wait_recv()
-        self.add_into(self.above, 0, [self.relayed])
-        self.near.append(
-            start(self.block(self.above, 0), self.landed(self.from_minus, 0), self.plus)
-        )
+        self.add_into(NEXT, 0, [self.relayed])
+        self.near.append(start(self.block(NEXT, 0), self.landed(self.from_before, 0), self.plus))
         self.far[1].wait_recv()
-        self.add_into(self.below, 1, [self.relayed])
-        self.near.append(
-            start(self.block(self.below, 1), self.landed(self.from_plus, 1), self.minus)
-        )
+        self.add_into(BEFORE, 1, [self.relayed])
+        self.near.append(start(self.block(BEFORE, 1), self.landed(self.from_next, 1), self.minus))
 
     def wait_near(self):
         for copy in self.near:
@@ -240,13 +232,33 @@
 
     def finish(self):
         self.wait_near()
-        self.add_into(self.pos[self.axis], None, [self.from_minus, self.from_plus])
+        self.add_into(0, None, [self.from_before, self.from_next])
 
     def finish_last(self):
         self.wait_near()
-        block = tuple(self.pos[axis] for axis in self.axes)
-        total = self.ref[block].astype(F32)
-        return total + self.from_minus[...].astype(F32) + self.from_plus[...].astype(F32)
+        total = self.ref[(0,) * len(self.axes)].astype(F32)
+        return total + self.from_before[...].astype(F32) + self.from_next[...].astype(F32)
+
+
+class Scatters:
+    def __init__(self, copies, pos, axes, ref, order, landing):
+        first, rest = order[0], order[1:]
+
+        def ring(phase, chosen):
+            later = [axis for axis in order[phase + 1 :] if isinstance(chosen[axis], tuple)]
+            even = [axis for axis in later if chosen[axis][1] % 2 == 0]
+            landing_axes = tuple(axis for axis in axes if axis in order[phase + 1 :])
+            one = Scatter(
+                copies, pos, ref, axes, order[phase], chosen, even[-1] if even else None
+            )
+            return one.land((landing_axes, landing[phase]))
+
+        whole = {axis: WHOLE for axis in rest}
+        self.portion = ring(0, {**whole, rest[0]: OTHERS})
+        self.remainder = ring(0, {**whole, rest[0]: 0})
+        self.second = ring(1, {first: 0, **{axis: WHOLE for axis in rest[1:]}})
+        self.third = ring(2, {first: 0, rest[0]: 0}) if len(rest) > 1 else None
+        self.last = self.third or self.second
 
 
 def landing_shapes(axis_count, rows, columns):
@@ -358,7 +370,7 @@
     hidden_in_copy.wait_recv()
     square_sum = jnp.zeros((CORES * rows, 1), F32)
     for (start, columns), scatter in zip(parts, scatters):
-        total = scatter.finish_last()
+        total = scatter.last.finish_last()
         total += residual[:, :, start : start + columns].reshape(CORES * rows, columns)
         attended = total.astype(BF16)
         attended_ref[:, start : start + columns] = attended
@@ -467,8 +479,6 @@
     landing_refs,
     final,
     final_in,
-    latent_send,
-    latent_recv,
     send_sems,
     recv_sems,
     local_sems,
@@ -486,6 +496,7 @@
     unit_count = gate_hbm.shape[2]
     shared_count = shared_gate_hbm.shape[0]
     expert_count = RING * CORES * RING
+    depth = CORES * unit_count + shared_count
     mine = pl.ds(pl.multiple_of(core * half, LANES), half)
     other = pl.ds(pl.multiple_of((1 - core) * half, LANES), half)
     own_units = pl.ds(pl.multiple_of(core * unit_count, unit_count), unit_count)
@@ -533,16 +544,6 @@
     )
     for copy in first_loads:
         copy.wait()
-
-    def latent_copy(peer):
-        return pltpu.make_async_remote_copy(
-            src_ref=latent_out.at[peer],
-            dst_ref=latents.at[inner],
-            send_sem=latent_send.at[peer],
-            recv_sem=latent_recv.at[inner],
-            device_id=(group, peer),
-            device_id_type=MESH,
-        )
 
     for chunk in range(2):
         query = queries[:, chunk * chunk_heads : (chunk + 1) * chunk_heads, :]
@@ -566,15 +567,16 @@
         latent_out[chunk * chunk_peers : (chunk + 1) * chunk_peers] = latent.reshape(
             chunk_peers, head_count * rows, latent_width
         )
-        if chunk == 0:
-            pl.semaphore_wait(barrier, len(partners))
-        for peer in range(chunk * chunk_peers, (chunk + 1) * chunk_peers):
-
-            @pl.when(inner != peer)
-            def _(peer=peer):
-                latent_copy(peer).start()
-
+    pl.semaphore_wait(barrier, len(partners))
     copies = Copies(send_sems, recv_sems)
+    arrivals = []
+    for place_x, place_y in sorted(
+        ((i, j) for i in range(RING) for j in range(RING) if i or j), reverse=True
+    ):
+        peer = moved(moved(pos, "x", OFFSETS[place_x]), "y", OFFSETS[place_y])
+        src = latent_out.at[peer["x"] * RING + peer["y"]]
+        dst = latents.at[FACING[place_x] * RING + FACING[place_y]]
+        arrivals.append(copies.start(src, dst, device_at(peer)))
     hidden_copy = copies.start(hidden_away, residual.at[core], sibling)
     late_loads = [
         load(gate_hbm.at[0, mine, :], inner_weights.at[2 * core]),
@@ -585,29 +587,9 @@
         load(shared_down_hbm.at[:, mine], down_weights.at[shared_units, :]),
     ]
 
-    def prepare(step, carry):
-        z, plane = lax.div(step, RING * RING), lax.rem(step, RING * RING)
-        x, y = lax.div(plane, RING), lax.rem(plane, RING)
-        for which in range(2 * CORES):
-            sums[which, z, x, y] = jnp.zeros((chip_rows, unit_count), F32)
-        hidden[z, x, y, :, CORES * unit_count :] = jnp.zeros((chip_rows, shared_count), BF16)
-        return carry
-
-    lax.fori_loop(0, RING**3, prepare, 0)
-
-    latents[inner] = latent_out[inner]
-    for peer in range(inner_count):
-
-        @pl.when(inner != peer)
-        def _(peer=peer):
-            pltpu.make_async_remote_copy(
-                src_ref=latent_out.at[peer],
-                dst_ref=latents.at[peer],
-                send_sem=latent_send.at[peer],
-                recv_sem=latent_recv.at[peer],
-                device_id=(group, peer),
-                device_id_type=MESH,
-            ).wait_recv()
+    latents[0] = latent_out[inner]
+    for copy in arrivals:
+        copy.wait_recv()
 
     for copy in head_loads:
         copy.wait()
@@ -634,24 +616,28 @@
     ):
         partial = nn_dot(heads, proj[:, start : start + columns])
         ref[...] = partial.astype(BF16).reshape(ref.shape)
-        scatter = Scatter(copies, pos, ("x", "y"), ref, order, by_phase(landing))
-        scatter.begin(0)
-        scatter.send_far()
-        scatter.send_near()
+        scatter = Scatters(copies, pos, ("x", "y"), ref, order, by_phase(landing))
+        scatter.portion.send_far()
+        scatter.portion.send_near()
         scatters.append(scatter)
     for scatter in scatters:
-        scatter.relay()
-    for scatter in scatters:
-        scatter.finish()
-        scatter.begin(1)
-        scatter.send_far()
-        scatter.send_near()
-    for scatter in scatters:
-        scatter.relay()
+        scatter.portion.relay()
+        scatter.remainder.send_far()
+        scatter.remainder.send_near()
+    for scatter in scatters:
+        scatter.portion.finish()
+        scatter.second.send_far()
+        scatter.second.send_near()
+    for scatter in scatters:
+        scatter.remainder.relay()
+    for scatter in scatters:
+        scatter.second.relay()
+    for scatter in scatters:
+        scatter.remainder.finish()
     hidden_copy.wait_recv()
     square_sum = jnp.zeros((chip_rows, 1), F32)
     for (start, columns), scatter in zip(plane_parts, scatters):
-        total = scatter.finish_last()
+        total = scatter.last.finish_last()
         total += residual[:, :, start : start + columns].reshape(chip_rows, columns)
         attended = total.astype(BF16)
         attended_rows[:, start : start + columns] = attended
@@ -666,69 +652,112 @@
 
     parts = column_parts(half, len(GATHER_ORDERS))
     for (start, columns), ref in zip(parts, row_refs):
-        ref[pos["z"], pos["x"], pos["y"], :, :columns] = normed[:, start : start + columns]
+        ref[0, 0, 0, :, :columns] = normed[:, start : start + columns]
     weighed = parts[1][1]
-    row_refs[1][pos["z"], pos["x"], pos["y"], :, weighed:] = in_three(
+    row_refs[1][0, 0, 0, :, weighed:] = in_three(
         residual[:, :, half:].reshape(chip_rows, LANES), expert_count
     )
-    gathers = [
-        Gather(copies, pos, ref, order) for ref, order in zip(row_refs, GATHER_ORDERS)
+
+    def gather_ring(ref, order, phase, ranges):
+        chosen = {axis: 0 for axis in AXES}
+        chosen.update(zip(order, ranges))
+        return Gather(copies, pos, ref, AXES, order[phase], chosen, order[0] if phase else None)
+
+    rings = [
+        (
+            gather_ring(ref, order, 0, ()),
+            gather_ring(ref, order, 1, (WHOLE,)),
+            gather_ring(ref, order, 2, (WHOLE, 0)),
+            gather_ring(ref, order, 2, (WHOLE, OTHERS)),
+        )
+        for ref, order in zip(row_refs, GATHER_ORDERS)
     ]
 
-    def multiply(which_part, place):
+    def multiply(which_part, places):
         start, columns = parts[which_part]
         ref = row_refs[which_part]
-        axis = GATHER_ORDERS[which_part][-1]
-        index = view_index(AXES, {axis: place}, None, None, columns)
+        chosen = {axis: WHOLE for axis in AXES}
+        chosen[GATHER_ORDERS[which_part][-1]] = places
+        index = view_index(AXES, chosen, None, None, columns)
+        spans = tuple(chosen[axis][1] for axis in AXES)
+        count = places[1] * plane_rows
 
         def one(which, carry):
-            block = ref[index[:-1] + (slice(0, columns),)].reshape(plane_rows, columns)
+            block = ref[index[:-1] + (slice(0, columns),)].reshape(count, columns)
             product = nn_dot(block, inner_weights[which, start : start + columns, :])
             at = (which,) + index
-            sums[at] = sums[at] + product.reshape(RING, RING, chip_rows, unit_count)
+            sums[at] = sums[at] + product.reshape(spans + (chip_rows, unit_count))
             return carry
 
         lax.fori_loop(0, 2 * CORES, one, 0)
 
-    for phase in range(3):
-        for gather in gathers:
-            gather.begin(phase)
-        last = phase == 2
-        if last:
-            for copy in late_loads:
-                copy.wait()
-            for copy in weight_copies:
-                copy.wait_recv()
-            for k, gather in enumerate(gathers):
-                multiply(k, pos[gather.axis])
-        for gather in gathers:
-            gather.relay()
-        for k, gather in enumerate(gathers):
-            gather.wait_near()
-            if last:
-                multiply(k, moved(pos, gather.axis, 1)[gather.axis])
-                multiply(k, moved(pos, gather.axis, -1)[gather.axis])
-        for k, gather in enumerate(gathers):
-            gather.wait_far()
-            if last:
-                multiply(k, moved(pos, gather.axis, 2)[gather.axis])
-
-    exchanges = []
-    for z in range(RING):
-
-        def narrow(step, carry):
-            which, plane = lax.div(step, RING * RING), lax.rem(step, RING * RING)
-            x, y = lax.div(plane, RING), lax.rem(plane, RING)
-            sums_out[which, z, x, y] = sums[which, z, x, y].astype(BF16)
-            return carry
-
-        lax.fori_loop(0, 2 * CORES * RING * RING, narrow, 0)
-        exchanges.append(copies.start(sums_out.at[:, z], sums_in.at[:, z], sibling))
+    for ring in rings:
+        ring[0].begin()
+
+    def prepare(places):
+        at = tuple(places[axis] for axis in AXES)
+        for which in range(2 * CORES):
+            sums[(which,) + at] = jnp.zeros((chip_rows, unit_count), F32)
+        hidden[at + (slice(None), slice(CORES * unit_count, depth))] = jnp.zeros(
+            (chip_rows, shared_count), BF16
+        )
+
+    over_blocks(AXES, {axis: WHOLE for axis in AXES}, None, None, prepare)
+    for ring in rings:
+        ring[0].relay()
+    for ring in rings:
+        ring[0].wait_near()
+        ring[0].wait_far()
+        ring[1].begin()
+    for ring in rings:
+        ring[2].begin()
+    for ring in rings:
+        ring[1].relay()
+    for copy in late_loads:
+        copy.wait()
+    for ring in rings:
+        ring[1].wait_near()
+        ring[1].wait_far()
+        ring[3].begin()
+    for ring in rings:
+        ring[2].relay()
+    for copy in weight_copies:
+        copy.wait_recv()
+    for k in range(len(rings)):
+        multiply(k, (0, 1))
+    for ring in rings:
+        ring[3].relay()
+    for k, ring in enumerate(rings):
+        ring[2].wait_near()
+        ring[3].wait_near()
+        multiply(k, (NEXT, 2))
+
+    def narrow(ranges):
+        chosen = dict(zip(AXES, ranges))
+
+        def one(places):
+            at = tuple(places[axis] for axis in AXES)
+            for which in range(2 * CORES):
+                sums_out[(which,) + at] = sums[(which,) + at].astype(BF16)
+
+        over_blocks(AXES, chosen, None, None, one)
+        index = (slice(None),) + view_index(AXES, chosen, None, None, unit_count)
+        return copies.start(sums_out.at[index], sums_in.at[index], sibling)
+
+    near, far = (0, FAR), (FAR, 1)
+    regions = [((z, 1), near, near) for z in range(FAR)]
+    regions += [(far, WHOLE, WHOLE), (near, far, WHOLE), (near, near, far)]
+    exchanges = [narrow(region) for region in regions[:FAR]]
+    for k, ring in enumerate(rings):
+        ring[2].wait_far()
+        ring[3].wait_far()
+        multiply(k, far)
+    exchanges += [narrow(region) for region in regions[FAR:]]
     for which in range(2):
         total = jnp.zeros((plane_rows, shared_count), F32)
         for (start, columns), ref in zip(parts, row_refs):
             total += nt_dot(
-                ref[pos["z"], :, :, :, :columns].reshape(plane_rows, columns),
+                ref[0, :, :, :, :columns].reshape(plane_rows, columns),
                 shared_weights[which, :, start : start + columns],
             )
         shared_sums[which] = total
@@ -740,78 +769,87 @@
     for z in range(RING):
         terms = row_refs[1][z, :, :, :, weighed:].reshape(plane_rows, LANES)
         row_scale[z] = nn_dot(terms, picks).reshape(RING, RING, chip_rows, CORES * LANES)
-    for z in range(RING):
-        exchanges[z].wait_recv()
-
-        def activate(plane, carry):
-            x, y = lax.div(plane, RING), lax.rem(plane, RING)
+    for region, exchange in zip(regions, exchanges):
+        exchange.wait_recv()
+
+        def activate(places):
+            at = tuple(places[axis] for axis in AXES)
             for which in range(CORES):
                 gate, up = (
-                    sums[2 * which + k, z, x, y] + sums_in[2 * which + k, z, x, y].astype(F32)
+                    sums[(2 * which + k,) + at] + sums_in[(2 * which + k,) + at].astype(F32)
                     for k in (0, 1)
                 )
-                scale = row_scale[z, x, y, :, which * LANES : (which + 1) * LANES]
+                lanes = slice(which * LANES, (which + 1) * LANES)
+                scale = row_scale[at + (slice(None), lanes)]
                 scale = jnp.concatenate([scale] * (unit_count // LANES), axis=1)
                 value = (silu(gate) * up * scale).astype(BF16)
-                hidden[z, x, y, :, which * unit_count : (which + 1) * unit_count] = value
-            return carry
-
-        lax.fori_loop(0, RING * RING, activate, 0)
+                units = slice(which * unit_count, (which + 1) * unit_count)
+                hidden[at + (slice(None), units)] = value
+
+        over_blocks(AXES, dict(zip(AXES, region)), None, None, activate)
     shared_copy.wait_recv()
     shared_gate_part, shared_up_part = (shared_sums[k] + shared_in[k] for k in (0, 1))
     shared_hidden = (silu(shared_gate_part) * shared_up_part).astype(BF16)
-    hidden[pos["z"], :, :, :, CORES * unit_count :] = shared_hidden.reshape(
+    hidden[0, :, :, :, CORES * unit_count :] = shared_hidden.reshape(
         RING, RING, chip_rows, shared_count
     )
 
     scatters = [
-        Scatter(copies, pos, AXES, ref, order, by_phase(landing))
+        Scatters(copies, pos, AXES, ref, order, by_phase(landing))
         for ref, order, landing in zip(part_refs, SCATTER_ORDERS, landing_refs)
     ]
 
-    def project(which_part, place):
+    def project(which_part, places):
         start, columns = parts[which_part]
-        scatter = scatters[which_part]
-        index = view_index(AXES, {scatter.axis: place}, None, None, columns)
+        chosen = {axis: WHOLE for axis in AXES}
+        chosen[SCATTER_ORDERS[which_part][0]] = places
+        index = view_index(AXES, chosen, None, None, columns)
+        spans = tuple(chosen[axis][1] for axis in AXES)
         product = nn_dot(
-            hidden[index].reshape(plane_rows, hidden.shape[-1]),
+            hidden[index].reshape(places[1] * plane_rows, depth),
             down_weights[:, start : start + columns],
         )
-        scatter.ref[index] = product.astype(BF16).reshape(RING, RING, chip_rows, columns)
+        part_refs[which_part][index] = product.astype(BF16).reshape(
+            spans + (chip_rows, columns)
+        )
 
     for k, scatter in enumerate(scatters):
-        scatter.begin(0)
-        project(k, scatter.across)
-        scatter.send_far()
+        project(k, far)
+        scatter.portion.send_far()
     for k, scatter in enumerate(scatters):
-        project(k, scatter.above)
-        project(k, scatter.below)
-        scatter.send_near()
-    for k, scatter in enumerate(scatters):
-        project(k, pos[scatter.axis])
-    for phase in range(2):
-        for scatter in scatters:
-            scatter.relay()
-        for scatter in scatters:
-            scatter.finish()
-            scatter.begin(phase + 1)
-            scatter.send_far()
-            scatter.send_near()
-    for scatter in scatters:
-        scatter.relay()
+        project(k, (NEXT, 1))
+        project(k, (BEFORE, 1))
+        scatter.portion.send_near()
+    for k in range(len(scatters)):
+        project(k, (0, 1))
+    for scatter in scatters:
+        scatter.portion.relay()
+    for scatter in scatters:
+        scatter.remainder.send_far()
+        scatter.remainder.send_near()
+    for scatter in scatters:
+        scatter.portion.finish()
+        scatter.second.send_far()
+        scatter.second.send_near()
+    for scatter in scatters:
+        scatter.remainder.relay()
+    for scatter in scatters:
+        scatter.second.relay()
+    for scatter in scatters:
+        scatter.remainder.finish()
+        scatter.second.finish()
+        scatter.third.send_far()
+        scatter.third.send_near()
+    for scatter in scatters:
+        scatter.third.relay()
     for (start, columns), scatter in zip(parts, scatters):
-        total = scatter.finish_last() + attended_rows[:, start : start + columns].astype(F32)
+        total = scatter.last.finish_last() + attended_rows[:, start : start + columns].astype(F32)
         final[:, :, start : start + columns] = total.reshape(CORES, rows, columns)
     final_copy = copies.start(final.at[1 - core], final_in, sibling)
     out_ref[:, mine] = final[core].astype(BF16)
     final_copy.wait_recv()
     out_ref[:, other] = final_in[...].astype(BF16)
     copies.finish()
-    for peer in range(inner_count):
-
-        @pl.when(inner != peer)
-        def _(peer=peer):
-            latent_copy(peer).wait_send()
 
 
 def local(
@@ -850,7 +888,7 @@
     vmem = pl.BlockSpec(memory_space=pltpu.VMEM)
     smem = pl.BlockSpec(memory_space=pltpu.SMEM)
     hbm = pl.BlockSpec(memory_space=pl.ANY)
-    copy_count = 2 * 2 * 6 + 3 * 3 * 6 * 2 + 3 + RING + 5
+    copy_count = inner_count - 1 + 6 * (2 * 3 + 3 * 4 * 2) + 6 + 3 + 5
     load_count = 10
     return pl.pallas_call(
         layer_kernel,
@@ -887,8 +925,6 @@
             [landing_shapes(3, chip_rows, columns) for _, columns in parts],
             pltpu.VMEM((CORES, rows, half), F32),
             pltpu.VMEM((rows, half), F32),
-            pltpu.SemaphoreType.DMA((inner_count,)),
-            pltpu.SemaphoreType.DMA((inner_count,)),
             pltpu.SemaphoreType.DMA((copy_count,)),
             pltpu.SemaphoreType.DMA((copy_count,)),
             pltpu.SemaphoreType.DMA((load_count,)),

time: 140 us -> 130 us (0.929)
  Pallas kernels: 138 us -> 127 us
    pallas_call x1, Pallas kernels: 138 us -> 127 us  [local(): pl.pallas_call(layer_kernel, out_shape=jax.ShapeDtypeStruct((rows, model_...]
where the time goes in v3:
time: 130 us
  Pallas kernels  127 us (98%)
  local copies, waits for them, and re-layouts  1.55 us (1%)
    pallas_call x1, Pallas kernels, local(): pl.pallas_call(layer_kernel, out_shape=jax.ShapeDtypeStruct((rows, model_...  127 us

profile of v3, /device:TPU:1, one launch (start us, length us, event | category | flops | bytes accessed | tf_op | source)
XLA Modules:
  0.0 129.6 jit_solution(10932791477543790946)
XLA Ops:
  0.7 127.3 %layer.1 = bf16[8,7168]{1,0:T(8,128)(2,1)} custom-call(s32[1]{0:T(128)S(6)} %copy.19.cache_len_ref, s32[1,8]{1,0:T(1,128)} %parents_ref.1, s32[8,8]{1,0:T(8,128)} %experts_ref.1, f32[8,8]{1,0:T(8,128)} %weights_ref.1, bf16[8,7168]{1,0:T(8,128)(2,1)} %hidden_ref.1, bf16[8,576]{1,0:T(8,128)(2,1)} %node_ref.1, f32[1,7168]{1,0:T(1,128)} %bitcast.7, ...), custom_call_target="tpu_custom_call" | custom-call | tf_op jit(solution)/shard_map/layer/pallas_call | solution.py:893
  128.0 1.6 %copy.20 = bf16[8,7168]{1,0:T(8,128)(2,1)} copy(bf16[8,7168]{1,0:T(8,128)(2,1)} %layer.1) | data formatting | bytes 229376

commit v4 on v3

--- a/solution.py
+++ b/solution.py
@@ -142,6 +142,7 @@
         self.chosen, self.split_axis = chosen, split_axis
         self.columns = ref.shape[-1]
         self.plus, self.minus = device_at(moved(pos, axis, 1)), device_at(moved(pos, axis, -1))
+        self.across = device_at(moved(pos, axis, 2))
 
     def block(self, place, half):
         chosen = dict(self.chosen)
@@ -165,6 +166,18 @@
         self.far = [start(block(BEFORE, 0), block(FAR, 0), self.plus)]
         self.first[1].wait_recv()
         self.far.append(start(block(NEXT, 1), block(FAR, 1), self.minus))
+
+    def send_direct(self):
+        start, block = self.copies.start, self.block
+        self.direct = [
+            start(block(0, None), block(FAR, None), self.across),
+            start(block(0, None), block(BEFORE, None), self.plus),
+            start(block(0, None), block(NEXT, None), self.minus),
+        ]
+
+    def wait_direct(self):
+        for copy in self.direct:
+            copy.wait_recv()
 
     def wait_near(self):
         self.first[2].wait_recv()
@@ -234,10 +247,20 @@
         self.wait_near()
         self.add_into(0, None, [self.from_before, self.from_next])
 
-    def finish_last(self):
-        self.wait_near()
+    def send_direct(self):
+        start = self.copies.start
+        self.direct = [
+            start(self.block(FAR, None), self.landed(self.relayed, None), self.across),
+            start(self.block(NEXT, None), self.landed(self.from_before, None), self.plus),
+            start(self.block(BEFORE, None), self.landed(self.from_next, None), self.minus),
+        ]
+
+    def finish_direct(self):
         total = self.ref[(0,) * len(self.axes)].astype(F32)
-        return total + self.from_before[...].astype(F32) + self.from_next[...].astype(F32)
+        for copy, ref in zip(self.direct, self.landing):
+            copy.wait_recv()
+            total += ref[...].astype(F32)
+        return total
 
 
 class Scatters:
@@ -271,118 +294,6 @@
 
 def by_phase(refs):
     return [refs[3 * k : 3 * k + 3] for k in range(len(refs) // 3)]
-
-
-def landing_shapes(axis_count, rows, columns):
-    shapes = []
-    for phase in range(axis_count):
-        lead = (RING,) * (axis_count - 1 - phase)
-        shapes += [pltpu.VMEM(lead + (rows, columns), BF16)] * 3
-    return shapes
-
-
-def by_phase(refs):
-    return [refs[3 * k : 3 * k + 3] for k in range(len(refs) // 3)]
-
-
-def attention_kernel(
-    latent_ref,
-    value_up_ref,
-    out_proj_hbm,
-    hidden_ref,
-    gain_ref,
-    attended_ref,
-    normed_ref,
-    latents,
-    proj,
-    head_out,
-    residual,
-    hidden_away,
-    squares,
-    squares_in,
-    part_refs,
-    landing_refs,
-    send_sems,
-    recv_sems,
-    local_sem,
-):
-    pos = my_position()
-    core, group, inner = pos["core"], lax.axis_index("group"), lax.axis_index("ingroup")
-    sibling = device_at(sibling_of(pos))
-    rows = hidden_ref.shape[0]
-    half = normed_ref.shape[1]
-    model_width = hidden_ref.shape[1]
-    inner_count = latent_ref.shape[0]
-    head_count, latent_width, value_width = value_up_ref.shape
-    mine = pl.ds(pl.multiple_of(core * half, LANES), half)
-    other = pl.ds(pl.multiple_of((1 - core) * half, LANES), half)
-    load_proj = pltpu.make_async_copy(out_proj_hbm.at[:, mine], proj, local_sem)
-    load_proj.start()
-    peers = [lax.rem(inner + step, inner_count) for step in range(1, inner_count)]
-    greet([(group, peer) for peer in peers] + [sibling])
-    copies = Copies(send_sems, recv_sems)
-
-    arrivals = [
-        copies.start(latent_ref.at[peer], latents.at[inner], (group, peer)) for peer in peers
-    ]
-    latents[inner] = latent_ref[inner]
-    hidden_away[...] = hidden_ref[:, other].astype(F32)
-    hidden_in_copy = copies.start(hidden_away, residual.at[core], sibling)
-    residual[core] = hidden_ref[:, mine].astype(F32)
-    for copy in arrivals:
-        copy.wait_recv()
-
-    stacked = latents[...].reshape(inner_count * head_count * rows, latent_width)
-    for head in range(head_count):
-        product = jnp.dot(stacked, value_up_ref[head], preferred_element_type=F32)
-        product = product.reshape(inner_count, head_count, rows, value_width)[:, head]
-        head_out[:, core, :, head * value_width : (head + 1) * value_width] = product.astype(
-            BF16
-        ).astype(F32)
-    heads_copy = copies.start(head_out.at[:, core], head_out.at[:, core], sibling)
-    load_proj.wait()
-    heads_copy.wait_recv()
-    heads = head_out[...].reshape(
-        inner_count * CORES * rows, head_count * value_width
-    ).astype(BF16)
-
-    parts = column_parts(half, len(PLANE_ORDERS))
-    scatters = []
-    for (start, columns), ref, landing, order in zip(
-        parts, part_refs, landing_refs, PLANE_ORDERS
-    ):
-        partial = jnp.dot(heads, proj[:, start : start + columns], preferred_element_type=F32)
-        ref[...] = partial.astype(BF16).reshape(ref.shape)
-        scatter = Scatter(copies, pos, ("x", "y"), ref, order, by_phase(landing))
-        scatter.begin(0)
-        scatter.send_far()
-        scatter.send_near()
-        scatters.append(scatter)
-    for scatter in scatters:
-        scatter.relay()
-    for scatter in scatters:
-        scatter.finish()
-        scatter.begin(1)
-        scatter.send_far()
-        scatter.send_near()
-    for scatter in scatters:
-        scatter.relay()
-    hidden_in_copy.wait_recv()
-    square_sum = jnp.zeros((CORES * rows, 1), F32)
-    for (start, columns), scatter in zip(parts, scatters):
-        total = scatter.last.finish_last()
-        total += residual[:, :, start : start + columns].reshape(CORES * rows, columns)
-        attended = total.astype(BF16)
-        attended_ref[:, start : start + columns] = attended
-        wide = attended.astype(F32)
-        square_sum += jnp.sum(wide * wide, axis=1, keepdims=True)
-    squares[...] = jnp.broadcast_to(square_sum, squares.shape)
-    squares_copy = copies.start(squares, squares_in, sibling)
-    squares_copy.wait_recv()
-    mean_square = (square_sum + squares_in[:, :1]) / model_width
-    scale = lax.rsqrt(mean_square + NORM_EPS)
-    normed_ref[...] = (attended_ref[...].astype(F32) * scale * gain_ref[:, mine]).astype(BF16)
-    copies.finish()
 
 
 def nt_dot(left, right):
@@ -501,6 +412,7 @@
     other = pl.ds(pl.multiple_of((1 - core) * half, LANES), half)
     own_units = pl.ds(pl.multiple_of(core * unit_count, unit_count), unit_count)
     shared_units = pl.ds(CORES * unit_count, shared_count)
+    gates, ups = pl.ds(0, unit_count), pl.ds(unit_count, unit_count)
 
     loads = []
 
@@ -514,7 +426,7 @@
     head_loads = [load(value_up_hbm, value_up), load(out_proj_hbm.at[:, mine], proj)]
 
     peers = [lax.rem(inner + step, inner_count) for step in range(1, inner_count)]
-    z_neighbours = [device_at(moved(pos, "z", by)) for by in (1, -1)]
+    z_neighbours = [device_at(moved(pos, "z", by)) for by in (1, -1, 2)]
     partners = [(group, peer) for peer in peers] + z_neighbours + [sibling]
     barrier = pltpu.get_barrier_semaphore()
     for partner in partners:
@@ -579,14 +491,23 @@
         arrivals.append(copies.start(src, dst, device_at(peer)))
     hidden_copy = copies.start(hidden_away, residual.at[core], sibling)
     late_loads = [
-        load(gate_hbm.at[0, mine, :], inner_weights.at[2 * core]),
-        load(up_hbm.at[0, mine, :], inner_weights.at[2 * core + 1]),
+        load(gate_hbm.at[0, mine, :], inner_weights.at[core, :, gates]),
+        load(up_hbm.at[0, mine, :], inner_weights.at[core, :, ups]),
         load(shared_gate_hbm.at[:, mine], shared_weights.at[0]),
         load(shared_up_hbm.at[:, mine], shared_weights.at[1]),
         load(down_hbm.at[0, :, mine], down_weights.at[own_units, :]),
         load(shared_down_hbm.at[:, mine], down_weights.at[shared_units, :]),
     ]
 
+    def prepare(places):
+        at = tuple(places[axis] for axis in AXES)
+        for which in range(CORES):
+            sums[(which,) + at] = jnp.zeros((chip_rows, 2 * unit_count), F32)
+        hidden[at + (slice(None), slice(CORES * unit_count, depth))] = jnp.zeros(
+            (chip_rows, shared_count), BF16
+        )
+
+    over_blocks(AXES, {axis: WHOLE for axis in AXES}, None, None, prepare)
     latents[0] = latent_out[inner]
     for copy in arrivals:
         copy.wait_recv()
@@ -603,8 +524,8 @@
     heads_copy = copies.start(head_out.at[:, core], head_out.at[:, core], sibling)
     heads_copy.wait_recv()
     weight_copies = [
-        copies.start(gate_hbm.at[0, other, :], inner_weights.at[2 * core], sibling),
-        copies.start(up_hbm.at[0, other, :], inner_weights.at[2 * core + 1], sibling),
+        copies.start(gate_hbm.at[0, other, :], inner_weights.at[core, :, gates], sibling),
+        copies.start(up_hbm.at[0, other, :], inner_weights.at[core, :, ups], sibling),
         copies.start(down_hbm.at[0, :, other], down_weights.at[own_units, :], sibling),
     ]
     heads = head_out[...].reshape(plane_rows, head_count * value_width).astype(BF16)
@@ -626,18 +547,15 @@
         scatter.remainder.send_near()
     for scatter in scatters:
         scatter.portion.finish()
-        scatter.second.send_far()
-        scatter.second.send_near()
+        scatter.second.send_direct()
     for scatter in scatters:
         scatter.remainder.relay()
-    for scatter in scatters:
-        scatter.second.relay()
     for scatter in scatters:
         scatter.remainder.finish()
     hidden_copy.wait_recv()
     square_sum = jnp.zeros((chip_rows, 1), F32)
     for (start, columns), scatter in zip(plane_parts, scatters):
-        total = scatter.last.finish_last()
+        total = scatter.last.finish_direct()
         total += residual[:, :, start : start + columns].reshape(chip_rows, columns)
         attended = total.astype(BF16)
         attended_rows[:, start : start + columns] = attended
@@ -686,33 +604,21 @@
             block = ref[index[:-1] + (slice(0, columns),)].reshape(count, columns)
             product = nn_dot(block, inner_weights[which, start : start + columns, :])
             at = (which,) + index
-            sums[at] = sums[at] + product.reshape(spans + (chip_rows, unit_count))
+            sums[at] = sums[at] + product.reshape(spans + (chip_rows, 2 * unit_count))
             return carry
 
-        lax.fori_loop(0, 2 * CORES, one, 0)
+        lax.fori_loop(0, CORES, one, 0)
 
     for ring in rings:
-        ring[0].begin()
-
-    def prepare(places):
-        at = tuple(places[axis] for axis in AXES)
-        for which in range(2 * CORES):
-            sums[(which,) + at] = jnp.zeros((chip_rows, unit_count), F32)
-        hidden[at + (slice(None), slice(CORES * unit_count, depth))] = jnp.zeros(
-            (chip_rows, shared_count), BF16
-        )
-
-    over_blocks(AXES, {axis: WHOLE for axis in AXES}, None, None, prepare)
+        ring[0].send_direct()
+
     for ring in rings:
-        ring[0].relay()
-    for ring in rings:
-        ring[0].wait_near()
-        ring[0].wait_far()
+        ring[0].wait_direct()
         ring[1].begin()
     for ring in rings:
+        ring[1].relay()
+    for ring in rings:
         ring[2].begin()
-    for ring in rings:
-        ring[1].relay()
     for copy in late_loads:
         copy.wait()
     for ring in rings:
@@ -737,7 +643,7 @@
 
         def one(places):
             at = tuple(places[axis] for axis in AXES)
-            for which in range(2 * CORES):
+            for which in range(CORES):
                 sums_out[(which,) + at] = sums[(which,) + at].astype(BF16)
 
         over_blocks(AXES, chosen, None, None, one)
@@ -775,10 +681,8 @@
         def activate(places):
             at = tuple(places[axis] for axis in AXES)
             for which in range(CORES):
-                gate, up = (
-                    sums[(2 * which + k,) + at] + sums_in[(2 * which + k,) + at].astype(F32)
-                    for k in (0, 1)
-                )
+                both = sums[(which,) + at] + sums_in[(which,) + at].astype(F32)
+                gate, up = both[:, :unit_count], both[:, unit_count:]
                 lanes = slice(which * LANES, (which + 1) * LANES)
                 scale = row_scale[at + (slice(None), lanes)]
                 scale = jnp.concatenate([scale] * (unit_count // LANES), axis=1)
@@ -838,12 +742,9 @@
     for scatter in scatters:
         scatter.remainder.finish()
         scatter.second.finish()
-        scatter.third.send_far()
-        scatter.third.send_near()
-    for scatter in scatters:
-        scatter.third.relay()
+        scatter.third.send_direct()
     for (start, columns), scatter in zip(parts, scatters):
-        total = scatter.last.finish_last() + attended_rows[:, start : start + columns].astype(F32)
+        total = scatter.last.finish_direct() + attended_rows[:, start : start + columns].astype(F32)
         final[:, :, start : start + columns] = total.reshape(CORES, rows, columns)
     final_copy = copies.start(final.at[1 - core], final_in, sibling)
     out_ref[:, mine] = final[core].astype(BF16)
@@ -911,13 +812,13 @@
             [pltpu.VMEM((RING, RING, chip_rows, columns), BF16) for _, columns in plane_parts],
             [landing_shapes(2, chip_rows, columns) for _, columns in plane_parts],
             [pltpu.VMEM(grid3 + (chip_rows, columns), BF16) for columns in gathered],
-            pltpu.VMEM((2 * CORES, half, unit_count), BF16),
+            pltpu.VMEM((CORES, half, 2 * unit_count), BF16),
             pltpu.VMEM((2, shared_count, half), BF16),
             pltpu.VMEM((depth, half), BF16),
             pltpu.VMEM(grid3 + (chip_rows, CORES * LANES), F32),
-            pltpu.VMEM((2 * CORES,) + grid3 + (chip_rows, unit_count), F32),
-            pltpu.VMEM((2 * CORES,) + grid3 + (chip_rows, unit_count), BF16),
-            pltpu.VMEM((2 * CORES,) + grid3 + (chip_rows, unit_count), BF16),
+            pltpu.VMEM((CORES,) + grid3 + (chip_rows, 2 * unit_count), F32),
+            pltpu.VMEM((CORES,) + grid3 + (chip_rows, 2 * unit_count), BF16),
+            pltpu.VMEM((CORES,) + grid3 + (chip_rows, 2 * unit_count), BF16),
             pltpu.VMEM((2, plane_rows, shared_count), F32),
             pltpu.VMEM((2, plane_rows, shared_count), F32),
             pltpu.VMEM(grid3 + (chip_rows, depth), BF16),

time: 130 us -> 123 us (0.946)
  Pallas kernels: 127 us -> 121 us
    pallas_call x1, Pallas kernels: 127 us -> 121 us  [local(): pl.pallas_call(layer_kernel, out_shape=jax.ShapeDtypeStruct((rows, model_...]
where the time goes in v4:
time: 123 us
  Pallas kernels  121 us (98%)
  local copies, waits for them, and re-layouts  1.55 us (1%)
    pallas_call x1, Pallas kernels, local(): pl.pallas_call(layer_kernel, out_shape=jax.ShapeDtypeStruct((rows, model_...  121 us

profile of v4, /device:TPU:1, one launch (start us, length us, event | category | flops | bytes accessed | tf_op | source)
XLA Modules:
  0.0 122.9 jit_solution(17640164829802619755)
XLA Ops:
  0.7 120.7 %layer.1 = bf16[8,7168]{1,0:T(8,128)(2,1)} custom-call(s32[1]{0:T(128)S(6)} %copy.19.cache_len_ref, s32[1,8]{1,0:T(1,128)} %parents_ref.1, s32[8,8]{1,0:T(8,128)} %experts_ref.1, f32[8,8]{1,0:T(8,128)} %weights_ref.1, bf16[8,7168]{1,0:T(8,128)(2,1)} %hidden_ref.1, bf16[8,576]{1,0:T(8,128)(2,1)} %node_ref.1, f32[1,7168]{1,0:T(1,128)} %bitcast.7, ...), custom_call_target="tpu_custom_call" | custom-call | tf_op jit(solution)/shard_map/layer/pallas_call | solution.py:794
  121.3 1.6 %copy.20 = bf16[8,7168]{1,0:T(8,128)(2,1)} copy(bf16[8,7168]{1,0:T(8,128)(2,1)} %layer.1) | data formatting | bytes 229376

commit v5 on v4

--- a/solution.py
+++ b/solution.py
@@ -15,9 +15,11 @@
 RING = 4
 CORES = 2
 LANES = 128
+SCALE_LANE = 96
 VMEM_LIMIT = 62 * 2**20
 AXES = ("z", "x", "y")
 GATHER_ORDERS = (("x", "y", "z"), ("y", "z", "x"), ("z", "x", "y"))
+TERMS_ORDER = ("z", "y", "x")
 SCATTER_ORDERS = (("z", "x", "y"), ("x", "y", "z"), ("y", "z", "x"))
 PLANE_ORDERS = (("x", "y"), ("y", "x"))
 
@@ -344,12 +346,12 @@
 
 def layer_kernel(
     cache_len_ref,
-    parents_ref,
-    experts_ref,
-    weights_ref,
     hidden_ref,
     node_ref,
-    gain_ref,
+    parents_hbm,
+    experts_hbm,
+    weights_hbm,
+    gain_hbm,
     queries_hbm,
     cache_hbm,
     value_up_hbm,
@@ -361,6 +363,10 @@
     shared_up_hbm,
     shared_down_hbm,
     out_ref,
+    parents_ref,
+    experts_ref,
+    weights_ref,
+    gain_ref,
     queries,
     cache,
     value_up,
@@ -376,6 +382,7 @@
     plane_refs,
     plane_landing,
     row_refs,
+    terms_ref,
     inner_weights,
     shared_weights,
     down_weights,
@@ -422,6 +429,12 @@
         loads.append(copy)
         return copy
 
+    small_loads = [
+        load(parents_hbm, parents_ref),
+        load(experts_hbm, experts_ref),
+        load(weights_hbm, weights_ref),
+        load(gain_hbm.at[:, mine], gain_ref),
+    ]
     first_loads = [load(queries_hbm, queries), load(cache_hbm.at[0], cache)]
     head_loads = [load(value_up_hbm, value_up), load(out_proj_hbm.at[:, mine], proj)]
 
@@ -432,6 +445,8 @@
     for partner in partners:
         pl.semaphore_signal(barrier, inc=1, device_id=partner, device_id_type=MESH)
 
+    for copy in small_loads:
+        copy.wait()
     routing = routing_lanes(experts_ref[...], weights_ref[...], expert_count)
     hidden_away[:, :half] = hidden_ref[:, other].astype(F32)
     hidden_away[:, half:] = routing
@@ -563,18 +578,11 @@
         square_sum += jnp.sum(wide * wide, axis=1, keepdims=True)
     squares[...] = jnp.broadcast_to(square_sum, squares.shape)
     squares_copy = copies.start(squares, squares_in, sibling)
-    squares_copy.wait_recv()
-    mean_square = (square_sum + squares_in[:, :1]) / model_width
-    scale = lax.rsqrt(mean_square + NORM_EPS)
-    normed = (attended_rows[...].astype(F32) * scale * gain_ref[:, mine]).astype(BF16)
-
     parts = column_parts(half, len(GATHER_ORDERS))
     for (start, columns), ref in zip(parts, row_refs):
-        ref[0, 0, 0, :, :columns] = normed[:, start : start + columns]
-    weighed = parts[1][1]
-    row_refs[1][0, 0, 0, :, weighed:] = in_three(
-        residual[:, :, half:].reshape(chip_rows, LANES), expert_count
-    )
+        span = slice(start, start + columns)
+        scaled = attended_rows[:, span].astype(F32) * gain_ref[:, span]
+        ref[0, 0, 0] = scaled.astype(BF16)
 
     def gather_ring(ref, order, phase, ranges):
         chosen = {axis: 0 for axis in AXES}
@@ -590,6 +598,9 @@
         )
         for ref, order in zip(row_refs, GATHER_ORDERS)
     ]
+    terms_rings = [
+        gather_ring(terms_ref, TERMS_ORDER, phase, (WHOLE,) * phase) for phase in range(3)
+    ]
 
     def multiply(which_part, places):
         start, columns = parts[which_part]
@@ -611,6 +622,21 @@
 
     for ring in rings:
         ring[0].send_direct()
+    squares_copy.wait_recv()
+    mean_square = (square_sum + squares_in[:, :1]) / model_width
+    scale = lax.rsqrt(mean_square + NORM_EPS)
+    routing_terms = in_three(residual[:, :, half:].reshape(chip_rows, LANES), expert_count)
+    lane = lax.broadcasted_iota(jnp.int32, (chip_rows, LANES), 1)
+    scale_high = scale.astype(BF16).astype(F32)
+    scale_middle = (scale - scale_high).astype(BF16).astype(F32)
+    scale_terms = jnp.where(
+        lane == SCALE_LANE,
+        scale_high,
+        jnp.where(lane == SCALE_LANE + 1, scale_middle, scale - scale_high - scale_middle),
+    )
+    is_scale = (lane >= SCALE_LANE) & (lane < SCALE_LANE + 3)
+    terms_ref[0, 0, 0] = jnp.where(is_scale, scale_terms, routing_terms.astype(F32)).astype(BF16)
+    terms_rings[0].send_direct()
 
     for ring in rings:
         ring[0].wait_direct()
@@ -619,6 +645,8 @@
         ring[1].relay()
     for ring in rings:
         ring[2].begin()
+    terms_rings[0].wait_direct()
+    terms_rings[1].send_direct()
     for copy in late_loads:
         copy.wait()
     for ring in rings:
@@ -627,13 +655,15 @@
         ring[3].begin()
     for ring in rings:
         ring[2].relay()
+    terms_rings[1].wait_direct()
+    terms_rings[2].send_direct()
     for copy in weight_copies:
         copy.wait_recv()
     for k in range(len(rings)):
         multiply(k, (0, 1))
     for ring in rings:
         ring[3].relay()
-    for k, ring in enumerate(rings):
+    for k, ring in reversed(list(enumerate(rings))):
         ring[2].wait_near()
         ring[3].wait_near()
         multiply(k, (NEXT, 2))
@@ -654,7 +684,7 @@
     regions = [((z, 1), near, near) for z in range(FAR)]
     regions += [(far, WHOLE, WHOLE), (near, far, WHOLE), (near, near, far)]
     exchanges = [narrow(region) for region in regions[:FAR]]
-    for k, ring in enumerate(rings):
+    for k, ring in reversed(list(enumerate(rings))):
         ring[2].wait_far()
         ring[3].wait_far()
         multiply(k, far)
@@ -668,13 +698,19 @@
             )
         shared_sums[which] = total
     shared_copy = copies.start(shared_sums, shared_in, sibling)
-    picks_from = lax.broadcasted_iota(jnp.int32, (LANES, CORES * LANES), 0)
-    picks_to = lax.div(lax.broadcasted_iota(jnp.int32, (LANES, CORES * LANES), 1), LANES)
-    chosen = (pos["z"] * CORES + picks_to) * RING + pos["x"]
-    picks = ((lax.rem(picks_from, expert_count) == chosen).astype(F32)).astype(BF16)
+    terms_rings[2].wait_direct()
+    picks_shape = (LANES, (CORES + 1) * LANES)
+    picks_from = lax.broadcasted_iota(jnp.int32, picks_shape, 0)
+    picks_to = lax.div(lax.broadcasted_iota(jnp.int32, picks_shape, 1), LANES)
+    chosen_expert = (pos["z"] * CORES + picks_to) * RING + pos["x"]
+    is_weight = (picks_from < SCALE_LANE) & (picks_to < CORES)
+    picked = (is_weight & (lax.rem(picks_from, expert_count) == chosen_expert)) | (
+        (picks_from >= SCALE_LANE) & (picks_to == CORES)
+    )
+    picks = picked.astype(F32).astype(BF16)
     for z in range(RING):
-        terms = row_refs[1][z, :, :, :, weighed:].reshape(plane_rows, LANES)
-        row_scale[z] = nn_dot(terms, picks).reshape(RING, RING, chip_rows, CORES * LANES)
+        terms = terms_ref[z].reshape(plane_rows, LANES)
+        row_scale[z] = nn_dot(terms, picks).reshape(RING, RING, chip_rows, (CORES + 1) * LANES)
     for region, exchange in zip(regions, exchanges):
         exchange.wait_recv()
 
@@ -682,6 +718,8 @@
             at = tuple(places[axis] for axis in AXES)
             for which in range(CORES):
                 both = sums[(which,) + at] + sums_in[(which,) + at].astype(F32)
+                norm = row_scale[at + (slice(None), slice(CORES * LANES, (CORES + 1) * LANES))]
+                both = both * jnp.concatenate([norm] * (2 * unit_count // LANES), axis=1)
                 gate, up = both[:, :unit_count], both[:, unit_count:]
                 lanes = slice(which * LANES, (which + 1) * LANES)
                 scale = row_scale[at + (slice(None), lanes)]
@@ -692,7 +730,11 @@
 
         over_blocks(AXES, dict(zip(AXES, region)), None, None, activate)
     shared_copy.wait_recv()
-    shared_gate_part, shared_up_part = (shared_sums[k] + shared_in[k] for k in (0, 1))
+    norm_lanes = slice(CORES * LANES, CORES * LANES + shared_count)
+    norm = row_scale[0, :, :, :, norm_lanes].reshape(plane_rows, shared_count)
+    shared_gate_part, shared_up_part = (
+        (shared_sums[k] + shared_in[k]) * norm for k in (0, 1)
+    )
     shared_hidden = (silu(shared_gate_part) * shared_up_part).astype(BF16)
     hidden[0, :, :, :, CORES * unit_count :] = shared_hidden.reshape(
         RING, RING, chip_rows, shared_count
@@ -784,19 +826,22 @@
     depth = CORES * unit_count + shared_count
     plane_parts = column_parts(half, len(PLANE_ORDERS))
     parts = column_parts(half, len(GATHER_ORDERS))
-    gathered = [columns + (LANES if k == 1 else 0) for k, (_, columns) in enumerate(parts)]
     grid3 = (RING, RING, RING)
     vmem = pl.BlockSpec(memory_space=pltpu.VMEM)
     smem = pl.BlockSpec(memory_space=pltpu.SMEM)
     hbm = pl.BlockSpec(memory_space=pl.ANY)
-    copy_count = inner_count - 1 + 6 * (2 * 3 + 3 * 4 * 2) + 6 + 3 + 5
-    load_count = 10
+    copy_count = inner_count - 1 + 9 + 6 * (2 * 3 + 3 * 4 * 2) + 6 + 3 + 5
+    load_count = 14
     return pl.pallas_call(
         layer_kernel,
         out_shape=jax.ShapeDtypeStruct((rows, model_width), BF16),
-        in_specs=[smem] + [vmem] * 6 + [hbm] * 10,
+        in_specs=[smem] + [vmem] * 2 + [hbm] * 14,
         out_specs=vmem,
         scratch_shapes=[
+            pltpu.VMEM(parents.shape, jnp.int32),
+            pltpu.VMEM(route_experts.shape, jnp.int32),
+            pltpu.VMEM(route_weights.shape, F32),
+            pltpu.VMEM((1, half), F32),
             pltpu.VMEM(queries.shape, BF16),
             pltpu.VMEM((cache.shape[2], cache.shape[1]), BF16),
             pltpu.VMEM(value_up.shape, BF16),
@@ -811,11 +856,12 @@
             pltpu.VMEM((chip_rows, half), BF16),
             [pltpu.VMEM((RING, RING, chip_rows, columns), BF16) for _, columns in plane_parts],
             [landing_shapes(2, chip_rows, columns) for _, columns in plane_parts],
-            [pltpu.VMEM(grid3 + (chip_rows, columns), BF16) for columns in gathered],
+            [pltpu.VMEM(grid3 + (chip_rows, columns), BF16) for _, columns in parts],
+            pltpu.VMEM(grid3 + (chip_rows, LANES), BF16),
             pltpu.VMEM((CORES, half, 2 * unit_count), BF16),
             pltpu.VMEM((2, shared_count, half), BF16),
             pltpu.VMEM((depth, half), BF16),
-            pltpu.VMEM(grid3 + (chip_rows, CORES * LANES), F32),
+            pltpu.VMEM(grid3 + (chip_rows, (CORES + 1) * LANES), F32),
             pltpu.VMEM((CORES,) + grid3 + (chip_rows, 2 * unit_count), F32),
             pltpu.VMEM((CORES,) + grid3 + (chip_rows, 2 * unit_count), BF16),
             pltpu.VMEM((CORES,) + grid3 + (chip_rows, 2 * unit_count), BF16),
@@ -836,11 +882,11 @@
         name="layer",
     )(
         cache_len,
+        hidden_in,
+        node_latent,
         parents,
         route_experts,
         route_weights,
-        hidden_in,
-        node_latent,
         ffn_gain.reshape(1, -1),
         queries,
         jnp.swapaxes(cache, 1, 2),

time: 123 us -> 120 us (0.976)
  Pallas kernels: 121 us -> 118 us
    pallas_call x1, Pallas kernels: 121 us -> 118 us  [local(): pl.pallas_call(layer_kernel, out_shape=jax.ShapeDtypeStruct((rows, model_...]
where the time goes in v5:
time: 120 us
  Pallas kernels  118 us (98%)
  local copies, waits for them, and re-layouts  1.55 us (1%)
    pallas_call x1, Pallas kernels, local(): pl.pallas_call(layer_kernel, out_shape=jax.ShapeDtypeStruct((rows, model_...  118 us

profile of v5, /device:TPU:1, one launch (start us, length us, event | category | flops | bytes accessed | tf_op | source)
XLA Modules:
  0.0 120.3 jit_solution(14045425605191206218)
XLA Ops:
  0.7 118.1 %layer.1 = bf16[8,7168]{1,0:T(8,128)(2,1)} custom-call(s32[1]{0:T(128)S(6)} %copy.19.cache_len_ref, bf16[8,7168]{1,0:T(8,128)(2,1)} %hidden_ref.1, bf16[8,576]{1,0:T(8,128)(2,1)} %node_ref.1, s32[1,8]{1,0:T(1,128)} %parents_hbm.1, s32[8,8]{1,0:T(8,128)} %experts_hbm.1, f32[8,8]{1,0:T(8,128)} %weights_hbm.1, f32[1,7168]{1,0:T(1,128)} %bitcast.7, ...), custom_call_target="tpu_custom_call" | custom-call | tf_op jit(solution)/shard_map/layer/pallas_call | solution.py:835
  118.8 1.6 %copy.20 = bf16[8,7168]{1,0:T(8,128)(2,1)} copy(bf16[8,7168]{1,0:T(8,128)(2,1)} %layer.1) | data formatting | bytes 229376

commit v6 on v5

--- a/solution.py
+++ b/solution.py
@@ -768,29 +768,35 @@
         scatter.portion.send_near()
     for k in range(len(scatters)):
         project(k, (0, 1))
-    for scatter in scatters:
+    late_last = scatters[::-1]
+    for scatter in late_last:
         scatter.portion.relay()
-    for scatter in scatters:
+    for scatter in late_last:
         scatter.remainder.send_far()
         scatter.remainder.send_near()
-    for scatter in scatters:
+    for scatter in late_last:
         scatter.portion.finish()
         scatter.second.send_far()
         scatter.second.send_near()
-    for scatter in scatters:
+    for scatter in late_last:
         scatter.remainder.relay()
-    for scatter in scatters:
+    for scatter in late_last:
         scatter.second.relay()
-    for scatter in scatters:
+    for scatter in late_last:
         scatter.remainder.finish()
         scatter.second.finish()
         scatter.third.send_direct()
-    for (start, columns), scatter in zip(parts, scatters):
+    final_copies = []
+    for (start, columns), scatter in list(zip(parts, scatters))[::-1]:
         total = scatter.last.finish_direct() + attended_rows[:, start : start + columns].astype(F32)
-        final[:, :, start : start + columns] = total.reshape(CORES, rows, columns)
-    final_copy = copies.start(final.at[1 - core], final_in, sibling)
+        span = pl.ds(start, columns)
+        final[:, :, span] = total.reshape(CORES, rows, columns)
+        final_copies.append(
+            copies.start(final.at[1 - core, :, span], final_in.at[:, span], sibling)
+        )
     out_ref[:, mine] = final[core].astype(BF16)
-    final_copy.wait_recv()
+    for copy in final_copies:
+        copy.wait_recv()
     out_ref[:, other] = final_in[...].astype(BF16)
     copies.finish()
 
@@ -830,7 +836,7 @@
     vmem = pl.BlockSpec(memory_space=pltpu.VMEM)
     smem = pl.BlockSpec(memory_space=pltpu.SMEM)
     hbm = pl.BlockSpec(memory_space=pl.ANY)
-    copy_count = inner_count - 1 + 9 + 6 * (2 * 3 + 3 * 4 * 2) + 6 + 3 + 5
+    copy_count = inner_count - 1 + 11 + 6 * (2 * 3 + 3 * 4 * 2) + 6 + 3 + 5
     load_count = 14
     return pl.pallas_call(
         layer_kernel,

time: 120 us -> 120 us (level)
  no operation moved by 1% of the time
where the time goes in v6:
time: 120 us
  Pallas kernels  118 us (98%)
  local copies, waits for them, and re-layouts  1.55 us (1%)
    pallas_call x1, Pallas kernels, local(): pl.pallas_call(layer_kernel, out_shape=jax.ShapeDtypeStruct((rows, model_...  118 us

profile of v6, /device:TPU:1, one launch (start us, length us, event | category | flops | bytes accessed | tf_op | source)
XLA Modules:
  0.0 120.3 jit_solution(8335743617445571531)
XLA Ops:
  0.7 118.1 %layer.1 = bf16[8,7168]{1,0:T(8,128)(2,1)} custom-call(s32[1]{0:T(128)S(6)} %copy.19.cache_len_ref, bf16[8,7168]{1,0:T(8,128)(2,1)} %hidden_ref.1, bf16[8,576]{1,0:T(8,128)(2,1)} %node_ref.1, s32[1,8]{1,0:T(1,128)} %parents_hbm.1, s32[8,8]{1,0:T(8,128)} %experts_hbm.1, f32[8,8]{1,0:T(8,128)} %weights_hbm.1, f32[1,7168]{1,0:T(1,128)} %bitcast.7, ...), custom_call_target="tpu_custom_call" | custom-call | tf_op jit(solution)/shard_map/layer/pallas_call | solution.py:841
  118.7 1.6 %copy.20 = bf16[8,7168]{1,0:T(8,128)(2,1)} copy(bf16[8,7168]{1,0:T(8,128)(2,1)} %layer.1) | data formatting | bytes 229376
